TPU v7x, 32 devices: a whole 2x2x4 slice. The times are simulated.
32 devices in a mesh: dom: 8 (over z, y), cls: 4 (over x, core).
Axes of the slice: x: 2, y: 2, z: 4, core: 2. Of those that a mesh axis runs over, the one named last changes fastest.
Arguments:
- images: bfloat16 [1024, 2048], P('dom'), may hold values from -70 to 70
- refs: bfloat16 [100, 12, 2048], P('cls'), may hold values from -0.41992188 to 0.41992188
- ctf: float32 [16, 1024], replicated, may hold values from 0.2 to 1
- inv_noise: float32 [16, 1024], replicated, may hold values from 0.3 to 3
- log_prior: float32 [100], P('cls'), may hold values from -4 to 4
- shifts: int32 [9, 2], replicated, may hold values from -4 to 4
- rot_prior: int32 [1024], P('dom'), may hold values from 0 to 11
- groups: int32 [1024], P('dom'), may hold values from 0 to 15
Outputs:
- new_refs: float32 [100, 24576], P('cls', 'dom')
- loglik: float32 [1024], P('dom')
- class_frac: float32 [100], P('cls')
All inputs are finite; a program needn't handle non-finite values.
Results may differ from a plain program's by a relative error of at most 0.005.
Values sent between devices are 32-bit elements; how exact they have to be, the bound alone decides.
No kernel may reach another device: no remote copies, remote signals or barrier semaphores. Data moves between devices by JAX's collectives and lax.ppermute only.
A program may use at most 128 MiB of HBM per device.

v0:
```python
import math

import jax
import jax.numpy as jnp
from jax import lax
from jax.sharding import PartitionSpec as P

HI = lax.Precision.HIGHEST


def phase_tables(shifts, fpix):
    side = int(math.isqrt(fpix))
    pos = jnp.arange(fpix, dtype=jnp.int32)
    freq_x = (pos % side).astype(jnp.float32)
    freq_y = (pos // side - side // 2).astype(jnp.float32)
    shift_f = shifts.astype(jnp.float32)
    angle = (
        2.0 * math.pi * (shift_f[:, 0:1] * freq_x[None] + shift_f[:, 1:2] * freq_y[None]) / 256.0
    )
    return (jnp.cos(angle), jnp.sin(angle))


def local(images, refs, ctf, inv_noise, log_prior, shifts, rot_prior, groups):
    count, two_f = images.shape
    fpix = two_f // 2
    classes, rots, _ = refs.shape
    ngroup = ctf.shape[0]
    nshift = shifts.shape[0]
    dom_n = lax.axis_size("dom")
    cw = ctf * inv_noise
    c2w = ctf * ctf * inv_noise
    cosine, sine = phase_tables(shifts, fpix)
    onehot = (groups[:, None] == jnp.arange(ngroup, dtype=jnp.int32)[None]).astype(jnp.float32)
    cw_img = jnp.dot(onehot, cw, precision=HI)
    real_part = images[:, :fpix].astype(jnp.float32)
    imag_part = images[:, fpix:].astype(jnp.float32)
    sr = real_part[:, None] * cosine[None] + imag_part[:, None] * sine[None]
    si = imag_part[:, None] * cosine[None] - real_part[:, None] * sine[None]
    copies = jnp.concatenate([sr * cw_img[:, None], si * cw_img[:, None]], axis=-1).astype(
        jnp.bfloat16
    )
    rows = copies.reshape(count * nshift, two_f)
    flat_refs = refs.reshape(classes * rots, two_f)
    cross = lax.dot_general(
        rows, flat_refs, (((1,), (1,)), ((), ())), preferred_element_type=jnp.float32
    )
    cross = cross.reshape(count, nshift, classes, rots)
    flat_f = flat_refs.astype(jnp.float32)
    power = flat_f[:, :fpix] ** 2 + flat_f[:, fpix:] ** 2
    norms = jnp.dot(c2w, power.T, precision=HI)
    norm_img = jnp.dot(onehot, norms, precision=HI).reshape(count, classes, rots)
    ridx = jnp.arange(rots, dtype=jnp.int32)
    gap = jnp.abs(ridx[None] - rot_prior[:, None])
    gap = jnp.minimum(gap, rots - gap).astype(jnp.float32)
    logp = (
        cross
        - 0.5 * norm_img[:, None]
        + log_prior[None, None, :, None]
        - (0.15 * gap * gap)[:, None, None, :]
    )
    local_peak = jnp.max(logp, axis=(1, 2, 3))
    peak = lax.pmax(local_peak, "cls")
    total = lax.psum(jnp.sum(jnp.exp(logp - peak[:, None, None, None]), axis=(1, 2, 3)), "cls")
    loglik = peak + jnp.log(total)
    post = jnp.exp(logp - loglik[:, None, None, None]).astype(jnp.bfloat16)
    per_img = jnp.sum(post.astype(jnp.float32), axis=1).reshape(count, classes * rots)
    local_mass = lax.dot_general(onehot, per_img, (((0,), (0,)), ((), ())), precision=HI)
    mass = lax.psum(local_mass, "dom")
    post_rows = post.reshape(count * nshift, classes, rots)
    width = two_f // dom_n
    full = jnp.einsum("nkr,nq->kqr", post_rows, rows, preferred_element_type=jnp.float32)
    num = lax.psum_scatter(
        full.reshape(classes, two_f * rots), "dom", scatter_dimension=1, tiled=True
    )
    c2w_two = jnp.concatenate([c2w, c2w], axis=1)
    c2w_part = lax.dynamic_slice_in_dim(c2w_two, lax.axis_index("dom") * width, width, 1)
    den = jnp.einsum("gkr,gq->kqr", mass.reshape(ngroup, classes, rots), c2w_part, precision=HI)
    new_refs = num / (den.reshape(classes, width * rots) + 1.0)
    class_frac = jnp.sum(mass.reshape(ngroup, classes, rots), axis=(0, 2)) / (count * dom_n)
    return (new_refs, loglik, class_frac)


def solution(mesh):
    return jax.shard_map(
        local,
        mesh=mesh,
        in_specs=(
            P("dom", None),
            P("cls", None, None),
            P(),
            P(),
            P("cls"),
            P(),
            P("dom"),
            P("dom"),
        ),
        out_specs=(P("cls", "dom"), P("dom"), P("cls")),
        check_vma=False,
    )
```

profile of v0, /device:TPU:0, one launch (start us, length us, event | category | flops | bytes accessed | tf_op | source)
XLA Modules:
  0.0 195.6 jit_solution(11185705169616977884)
XLA Ops:
  7.2 0.0 reduce-scatter.2.cloned.1.call-start
  7.2 0.0 copy-start.5
  7.2 0.8 convert_element_type.47
  8.0 0.7 multiply_multiply_fusion.1
  8.7 0.9 multiply_multiply_fusion
  9.6 2.1 %fusion.16 = f32[128,1024]{1,0:T(8,128)} fusion(f32[16,1024]{1,0:T(8,128)} %param.10, f32[16,1024]{1,0:T(8,128)} %param.11, s32[128]{0:T(128)} %param.15), kind=kOutput, calls=%fused_computation.25 | convolution fusion | flops 25184256 | bytes 655872 | tf_op jit(solution)/shard_map/dot_general | solution.py:34
  11.7 2.1 %slice_convert_fusion.1 = (f32[128,1024]{1,0:T(8,128)}, f32[128,1024]{1,0:T(8,128)}) fusion(bf16[128,2048]{1,0:T(8,128)(2,1)} %param.8), kind=kLoop, calls=%fused_computation.21 | loop fusion | flops 262144 | bytes 1572864 | tf_op jit(solution)/shard_map/convert_element_type | solution.py:35
  13.8 0.0 copy-done.5
  13.8 0.8 copy.20
  14.6 0.0 copy-start.7
  14.6 1.7 reshape.216
  16.3 2.9 %fusion.13 = f32[16,300]{1,0:T(8,128)S(1)} fusion(f32[16,1024]{1,0:T(8,128)S(1)} %multiply_multiply_fusion, f32[300,2048]{1,0:T(8,128)} %reshape.216), kind=kOutput, calls=%fused_computation.15 | convolution fusion | flops 59904000 | bytes 2542336 | tf_op jit(solution)/shard_map/dot_general | solution.py:50
  19.3 0.0 copy-done.7
  19.3 0.3 convolution_multiply_fusion
  19.7 0.1 copy.21
  19.8 0.3 fusion.20
  20.1 0.0 copy-done.2
  20.1 0.0 copy-done.3
  20.1 0.0 copy-done.4
  20.1 0.0 copy-start.6
  20.1 0.0 copy-start.9
  20.1 1.6 multiply_convert_fusion.1
  21.7 0.0 copy-start
  21.8 0.0 copy-start.1
  21.8 0.0 copy-done.6
  21.8 0.0 copy-done.9
  21.8 2.3 %fusion.42 = (f32[128]{0:T(128)S(1)}, f32[128,9,25,12]{0,2,3,1:T(8,128)S(1)}) fusion(f32[128,12]{0,1:T(8,128)S(1)} %multiply_multiply_fusion.1, f32[25]{0:T(128)S(1)} %copy-done.9, f32[128,25,12]{0,1,2:T(8,128)S(1)} %copy.21, bf16[25,12,2048]{2,0,1:T(8,128)(2,1)S(1)} %copy-done.6, bf16[128,9,1024]{2,0,1:T(8,128)(2,1)S(1)} %get-tuple-element.4, ...), kind=kOutput, calls=%fused_computation.62 | convolution fusion | flops 1426397056 | bytes 7490148 | tf_op jit(solution)/shard_map/dot_general | solution.py:44
  24.1 8.3 %pmax.7 = f32[128]{0:T(128)S(1)} all-reduce(f32[128]{0:T(128)S(1)} %get-tuple-element.11), channel_id=1, replica_groups=mesh['dom'=8,'cls'=4] {'cls'}, use_global_device_ids=true, to_apply=%region_1.2 | all-reduce | flops 128 | bytes 1024 | tf_op jit(solution)/shard_map/pmax | solution.py:62
  32.5 0.5 exponential_reduce_fusion
  33.0 5.9 %psum.14 = f32[128]{0:T(128)S(1)} all-reduce(f32[128]{0:T(128)S(1)} %exponential_reduce_fusion), channel_id=1, replica_groups=mesh['dom'=8,'cls'=4] {'cls'}, use_global_device_ids=true, to_apply=%region_3.4 | all-reduce | flops 128 | bytes 1024 | tf_op jit(solution)/shard_map/psum | solution.py:63
  38.9 6.2 %fusion.4 = f32[25,2048,12]{1,0,2:T(8,128)} fusion(bf16[128,9,1024]{2,0,1:T(8,128)(2,1)} %copy-done.1, bf16[128,9,1024]{2,0,1:T(8,128)(2,1)} %copy-done, f32[128,9,25,12]{0,2,3,1:T(8,128)S(1)} %get-tuple-element.12, f32[128]{0:T(128)S(1)} %log_add_fusion), kind=kOutput, calls=%fused_computation.7 | convolution fusion | flops 1425705984 | bytes 8559104 | tf_op jit(solution)/shard_map/nkr,nq->kqr/dot_general | solution.py:71
  45.1 16.5 %copy.23 = f32[25,2048,12]{2,1,0:T(8,128)} copy(f32[25,2048,12]{1,0,2:T(8,128)} %fusion.4) | data formatting | bytes 4915200 | tf_op jit(solution)/shard_map/nkr,nq->kqr/transpose | solution.py:71
  61.7 49.8 %reshape.213 = f32[25,24576]{1,0:T(8,128)} reshape(f32[25,2048,12]{2,1,0:T(8,128)} %copy.23) | data formatting | bytes 4915200 | tf_op jit(solution)/shard_map/reshape | solution.py:73
  111.5 0.0 reduce-scatter.2.cloned.1.call-update
  111.5 0.3 convert_reduce_fusion
  111.8 0.1 copy.24
  111.9 0.3 fusion.21
  112.2 38.6 %psum.15 = f32[16,300]{1,0:T(8,128)S(1)} all-reduce(f32[16,300]{1,0:T(8,128)S(1)} %fusion.21), channel_id=1, replica_groups=mesh['dom'=8,'cls'=4] {'dom'}, use_global_device_ids=true, to_apply=%region_6.7 | all-reduce | flops 4800 | bytes 38400 | tf_op jit(solution)/shard_map/psum | solution.py:68
  150.8 0.2 reshape.215
  151.0 0.1 reduce_sum.37
  151.1 0.1 reduce_sum.38
  151.2 0.2 copy.25
  151.5 1.3 fusion.15
  152.7 2.0 %copy.26 = f32[25,256,12]{2,1,0:T(8,128)S(1)} copy(f32[25,256,12]{1,0,2:T(8,128)} %fusion.15) | data formatting | bytes 614400 | tf_op jit(solution)/shard_map/add | solution.py:78
  154.7 3.7 %add.79 = f32[25,3072]{1,0:T(8,128)} reshape(f32[25,256,12]{2,1,0:T(8,128)S(1)} %copy.26) | data formatting | bytes 614400 | tf_op jit(solution)/shard_map/add | solution.py:78
  158.4 0.5 broadcast_multiply_fusion
  158.9 27.9 %reduce-scatter.2.cloned.1.call-done = f32[25,3072]{1,0:T(8,128)} async-done(((f32[25,24576]{1,0:T(8,128)}), f32[25,3072]{1,0:T(8,128)}) %reduce-scatter.2.cloned.1.call-update) | async-done | bytes 307216 | tf_op jit(solution)/shard_map/reduce_scatter | solution.py:72
  186.9 1.9 div.24
  (13 shorter events, 0.1 us)
Async XLA Ops:
  7.2 179.7 %reduce-scatter.2.cloned.1.call-start = ((), (), s32[]{:S(2)}) async-start(), calls=%async_computation.1 | async-start | bytes 3538944 | tf_op jit(solution)/shard_map/reduce_scatter | solution.py:72
  7.2 6.6 %copy-start.5 = (bf16[25,12,2048]{2,0,1:T(8,128)(2,1)S(1)}, bf16[25,12,2048]{2,0,1:T(8,128)(2,1)}, u32[]{:S(2)}) copy-start(bf16[25,12,2048]{2,0,1:T(8,128)(2,1)} %param.9) | copy-start | bytes 3686404
  14.6 4.7 %copy-start.7 = (s32[128]{0:T(128)S(1)}, s32[128]{0:T(128)}, u32[]{:S(2)}) copy-start(s32[128]{0:T(128)} %param.15) | copy-start | bytes 1540
  16.3 3.8 %copy-start.2 = (f32[128,1024]{1,0:T(8,128)S(1)}, f32[128,1024]{1,0:T(8,128)}, u32[]{:S(2)}) copy-start(f32[128,1024]{1,0:T(8,128)} %get-tuple-element.5) | copy-start | bytes 1572868
  16.3 3.8 %copy-start.3 = (f32[128,1024]{1,0:T(8,128)S(1)}, f32[128,1024]{1,0:T(8,128)}, u32[]{:S(2)}) copy-start(f32[128,1024]{1,0:T(8,128)} %get-tuple-element.6) | copy-start | bytes 1572868
  16.3 3.8 %copy-start.4 = (f32[128,1024]{1,0:T(8,128)S(1)}, f32[128,1024]{1,0:T(8,128)}, u32[]{:S(2)}) copy-start(f32[128,1024]{1,0:T(8,128)} %fusion.16) | copy-start | bytes 1572868
  20.1 1.7 copy-start.6
  20.1 1.6 copy-start.9
  21.7 2.4 %copy-start = (bf16[128,9,1024]{2,0,1:T(8,128)(2,1)}, bf16[128,9,1024]{2,0,1:T(8,128)(2,1)S(1)}, u32[]{:S(2)}) copy-start(bf16[128,9,1024]{2,0,1:T(8,128)(2,1)S(1)} %get-tuple-element.3) | copy-start | bytes 7077892
  21.8 2.4 %copy-start.1 = (bf16[128,9,1024]{2,0,1:T(8,128)(2,1)}, bf16[128,9,1024]{2,0,1:T(8,128)(2,1)S(1)}, u32[]{:S(2)}) copy-start(bf16[128,9,1024]{2,0,1:T(8,128)(2,1)S(1)} %get-tuple-element.4) | copy-start | bytes 7077892
  38.9 72.6 %copy-start.8 = (f32[128]{0:T(128)}, f32[128]{0:T(128)S(1)}, u32[]{:S(2)}) copy-start(f32[128]{0:T(128)S(1)} %log_add_fusion) | copy-start | bytes 1540
Sparse Core Ops, SparseCore 0:
  111.6 75.2 reduce-scatter.1
where the time goes:
time: 196 us
  local copies, waits for them, and re-layouts  75.3 us (38%)
  blocking collectives  52.9 us (27%)
  waiting for transfers between devices  28 us (14%)
  matrix products  15.5 us (8%)
  between operations  14.3 us (7%)
  other arithmetic  9.7 us (5%)
    reshape x1, local copies, waits for them, and re-layouts, local(): full.reshape(classes, two_f * rots)  49.8 us
    psum x1, blocking collectives, local(): mass = lax.psum(local_mass, 'dom')  38.6 us
    reduce_scatter x1, waiting for transfers between devices, local(): lax.psum_scatter(full.reshape(classes, two_f * rots), 'dom', scatter_dime...  27.9 us
    transpose x1, local copies, waits for them, and re-layouts, local(): jnp.einsum('nkr,nq->kqr', post_rows, rows, preferred_element_type=jnp.flo...  16.5 us
    pmax x1, blocking collectives, local(): peak = lax.pmax(local_peak, 'cls')  8.34 us
    dot_general x1, matrix products, local(): jnp.einsum('nkr,nq->kqr', post_rows, rows, preferred_element_type=jnp.flo...  6.21 us
    psum x1, blocking collectives, local(): lax.psum(jnp.sum(jnp.exp(logp - peak[:, None, None, None]), axis=(1, 2, 3...  5.93 us
    add x2, local copies, waits for them, and re-layouts, local(): new_refs = num / (den.reshape(classes, width * rots) + 1.0)  5.66 us
  transfers between devices with their start and end apart: 1, of which 1 were waited for; matrix products, arithmetic and copies ran while one was open for 4% of the time, Pallas kernels for 0%

commit v1 on v0

v1 whole, which is shorter than its diff:
```python
import math

import jax
import jax.numpy as jnp
from jax import lax
from jax.experimental import pallas as pl
from jax.experimental.pallas import tpu as pltpu
from jax.sharding import PartitionSpec as P

HI = lax.Precision.HIGHEST
F32 = jnp.float32
BF16 = jnp.bfloat16
VMEM = pl.BlockSpec(memory_space=pltpu.VMEM)
HBM = pl.BlockSpec(memory_space=pltpu.HBM)
PARAMS = pltpu.CompilerParams(vmem_limit_bytes=20 * 1024 * 1024)
LOW = -1e30


def round_up(value, multiple):
    return -(-value // multiple) * multiple


def thirds(value, axis):
    high = value.astype(BF16)
    rest = value - high.astype(F32)
    middle = rest.astype(BF16)
    low = (rest - middle.astype(F32)).astype(BF16)
    return jnp.concatenate([high, middle, low], axis=axis)


def estep_kernel(
    images_hbm, refs_hbm, ctf_hbm, inv_hbm, prior_hbm, shifts_hbm, rot_hbm, groups_hbm,
    weight_ref, copies_ref, stats_ref, onehot_ref, share_ref,
    images_ref, refs_ref, ctf_ref, inv_ref, prior_ref, shifts_ref, rot_ref, groups_ref,
    flat_ref, flat_bf_ref, cw_ref, cos_ref, sin_ref, sems,
):
    count, two_f = images_ref.shape
    fpix = two_f // 2
    rots, classes, _ = refs_ref.shape
    ngroup = ctf_ref.shape[0]
    nshift = shifts_ref.shape[1]
    rpad = flat_ref.shape[0]
    half = classes * rots // 2
    hpad = rpad // 2

    loads = [
        pltpu.make_async_copy(src, dst, sems.at[index])
        for index, (src, dst) in enumerate(
            (
                (shifts_hbm, shifts_ref),
                (groups_hbm, groups_ref),
                (ctf_hbm, ctf_ref),
                (inv_hbm, inv_ref),
                (images_hbm, images_ref),
                (refs_hbm, refs_ref),
                (prior_hbm, prior_ref),
                (rot_hbm, rot_ref),
            )
        )
    ]
    for load in loads:
        load.start()
    side = int(math.isqrt(fpix))
    pos = lax.broadcasted_iota(jnp.int32, (1, fpix), 1).astype(F32)
    line = jnp.floor((pos + 0.5) * (1.0 / side))
    freq_x = pos - side * line
    freq_y = line - side // 2
    loads[0].wait()
    index = lax.broadcasted_iota(jnp.int32, (cos_ref.shape[0], 1), 0)
    shift_x = jnp.zeros(index.shape, F32)
    shift_y = jnp.zeros(index.shape, F32)
    for s in range(nshift):
        shift_x = jnp.where(index == s, shifts_ref[0, s].astype(F32), shift_x)
        shift_y = jnp.where(index == s, shifts_ref[1, s].astype(F32), shift_y)
    angle = 2.0 * math.pi * (shift_x * freq_x + shift_y * freq_y) / 256.0
    cos_ref[...] = jnp.cos(angle)
    sin_ref[...] = jnp.sin(angle)

    for load in loads[1:4]:
        load.wait()
    own = groups_ref[...].reshape(1, count)
    onehot = (own == lax.broadcasted_iota(jnp.int32, (ngroup, count), 0)).astype(F32)
    onehot_ref[...] = onehot
    three = jnp.concatenate([onehot] * 3, axis=0).astype(BF16)
    weight = ctf_ref[...] * inv_ref[...]
    cw_ref[...] = lax.dot_general(
        three, thirds(weight, 0), (((0,), (0,)), ((), ())), preferred_element_type=F32
    )
    loads[4].wait()

    def build(shifts):
        for at in range(0, count, 16):
            for lane in range(0, fpix, 128):
                real = images_ref[at : at + 16, lane : lane + 128].astype(F32)
                imag = images_ref[at : at + 16, fpix + lane : fpix + lane + 128].astype(F32)
                cw = cw_ref[at : at + 16, lane : lane + 128]
                for s in shifts:
                    c = cos_ref[s : s + 1, lane : lane + 128]
                    d = sin_ref[s : s + 1, lane : lane + 128]
                    to = s * count + at
                    copies_ref[to : to + 16, lane : lane + 128] = (
                        (real * c + imag * d) * cw
                    ).astype(BF16)
                    copies_ref[to : to + 16, fpix + lane : fpix + lane + 128] = (
                        (imag * c - real * d) * cw
                    ).astype(BF16)

    for load in loads[5:]:
        load.wait()
    for side in range(2):
        flat_ref[side * hpad + half : (side + 1) * hpad, :] = jnp.zeros((hpad - half, two_f), F32)
        for r in range(rots // 2):
            at = side * hpad + r * classes
            flat_ref[at : at + classes, :] = refs_ref[side * (rots // 2) + r].astype(F32)
    power = flat_ref[:, :fpix] ** 2 + flat_ref[:, fpix:] ** 2
    c2w = ctf_ref[...] * ctf_ref[...] * inv_ref[...]
    high = power.astype(BF16)
    low = (power - high.astype(F32)).astype(BF16)
    c2w = thirds(c2w, 0)
    norms = lax.dot_general(
        high, c2w, (((1,), (1,)), ((), ())), preferred_element_type=F32
    ) + lax.dot_general(low, c2w, (((1,), (1,)), ((), ())), preferred_element_type=F32)
    norms = norms[:, :ngroup] + norms[:, ngroup : 2 * ngroup] + norms[:, 2 * ngroup :]
    norm_img = jnp.dot(thirds(norms, 1), three, preferred_element_type=F32)
    row = lax.broadcasted_iota(jnp.int32, (rpad, 1), 0)
    row = jnp.where(row < hpad, row, row - hpad + half)
    valid = (row < half) | ((row >= half) & (lax.broadcasted_iota(jnp.int32, (rpad, 1), 0) >= hpad))
    valid = valid & (row < 2 * half)
    row = row.astype(F32)
    rot = jnp.floor((row + 0.5) * (1.0 / classes))
    lane = lax.broadcasted_iota(jnp.int32, (rpad, classes), 1).astype(F32)
    own = jnp.where(lane == row - rot * classes, prior_ref[...].reshape(1, classes), 0.0)
    prior = jnp.sum(own, axis=1, keepdims=True)
    gap = jnp.abs(rot - rot_ref[...].reshape(1, count).astype(F32))
    gap = jnp.minimum(gap, rots - gap)
    bias = prior - 0.5 * norm_img - 0.15 * gap * gap
    bias = jnp.where(valid, bias, LOW)

    flat_bf_ref[...] = flat_ref[...].astype(BF16)
    total = nshift * count
    pairs = [list(range(s, min(s + 4, nshift))) for s in range(0, nshift, 4)]
    peak = None
    build(pairs[0])
    for index, shifts in enumerate(pairs):
        if index + 1 < len(pairs):
            build(pairs[index + 1])
        at = shifts[0] * count
        cross = lax.dot_general(
            flat_bf_ref[...], copies_ref[at : at + len(shifts) * count, :], (((1,), (1,)), ((), ())),
            preferred_element_type=F32,
        )
        for sub in range(0, len(shifts) * count, count):
            logp = cross[:, sub : sub + count] + bias
            weight_ref[:, at + sub : at + sub + count] = logp
            top = jnp.max(logp, axis=0, keepdims=True)
            peak = top if peak is None else jnp.maximum(peak, top)
    mass = jnp.zeros((rpad, count), F32)
    for at in range(0, total, count):
        value = jnp.exp(weight_ref[:, at : at + count] - peak)
        weight_ref[:, at : at + count] = value
        mass = mass + value
    stats_ref[0:1, :] = peak
    stats_ref[1:2, :] = jnp.sum(mass, axis=0, keepdims=True)

    width = share_ref.shape[1]
    if width % 128 == 0:
        start = pl.multiple_of(lax.rem(lax.axis_index("dom") * width, fpix), width)
        share_ctf = ctf_ref[:, pl.ds(start, width)]
        share_ref[...] = share_ctf * share_ctf * inv_ref[:, pl.ds(start, width)]


def estep(images, refs, ctf, inv_noise, log_prior, shifts, rot_prior, groups, rpad, width):
    count, two_f = images.shape
    ngroup, fpix = ctf.shape
    nshift = shifts.shape[0]
    refs = jnp.swapaxes(refs, 0, 1)
    shifts = shifts.T
    return pl.pallas_call(
        estep_kernel,
        out_shape=(
            jax.ShapeDtypeStruct((rpad, nshift * count), F32),
            jax.ShapeDtypeStruct((nshift * count, two_f), BF16),
            jax.ShapeDtypeStruct((2, count), F32),
            jax.ShapeDtypeStruct((ngroup, count), F32),
            jax.ShapeDtypeStruct((ngroup, width), F32),
        ),
        in_specs=[HBM] * 8,
        out_specs=(VMEM,) * 5,
        scratch_shapes=[
            pltpu.VMEM(images.shape, images.dtype),
            pltpu.VMEM(refs.shape, refs.dtype),
            pltpu.VMEM(ctf.shape, F32),
            pltpu.VMEM(ctf.shape, F32),
            pltpu.VMEM(log_prior.shape, F32),
            pltpu.SMEM(shifts.shape, jnp.int32),
            pltpu.VMEM(rot_prior.shape, jnp.int32),
            pltpu.VMEM(groups.shape, jnp.int32),
            pltpu.VMEM((rpad, two_f), F32),
            pltpu.VMEM((rpad, two_f), BF16),
            pltpu.VMEM((count, fpix), F32),
            pltpu.VMEM((round_up(nshift, 8), fpix), F32),
            pltpu.VMEM((round_up(nshift, 8), fpix), F32),
            pltpu.SemaphoreType.DMA((8,)),
        ],
        compiler_params=PARAMS,
        name="estep",
    )(
        *(
            pltpu.with_memory_space_constraint(value, pltpu.HBM)
            for value in (images, refs, ctf, inv_noise, log_prior, shifts, rot_prior, groups)
        )
    )


def posterior(stats_refs, weight_ref, onehot_ref, post_ref, loglik_ref):
    count = onehot_ref.shape[1]
    parts = len(stats_refs)
    me = lax.axis_index("cls")
    stats = [ref[...] for ref in stats_refs]
    ordered = []
    for place in range(parts):
        value = stats[0]
        for ahead in range(1, parts):
            value = jnp.where(lax.rem(me + ahead, parts) == place, stats[ahead], value)
        ordered.append(value)
    peak = ordered[0][0:1]
    for value in ordered[1:]:
        peak = jnp.maximum(peak, value[0:1])
    total = jnp.zeros_like(peak)
    for value in ordered:
        total = total + value[1:2] * jnp.exp(value[0:1] - peak)
    loglik = peak + jnp.log(total)
    scale = jnp.exp(stats[0][0:1] - loglik)
    loglik_ref[...] = loglik.reshape(count)
    per_img = None
    for at in range(0, weight_ref.shape[1], count):
        post = (weight_ref[:, at : at + count] * scale).astype(BF16)
        post_ref[:, at : at + count] = post
        post = post.astype(F32)
        per_img = post if per_img is None else per_img + post
    three = jnp.concatenate([onehot_ref[...]] * 3, axis=1).astype(BF16)
    hpad = per_img.shape[0] // 2
    return [
        lax.dot_general(
            three, thirds(per_img[at : at + hpad], 1), (((1,), (1,)), ((), ())),
            preferred_element_type=F32,
        )
        for at in (0, hpad)
    ]


def class_sums(post_ref, copies_ref, rows, at, width):
    return jnp.dot(post_ref[rows, :], copies_ref[:, pl.ds(at, width)], preferred_element_type=F32)


LINE = 4
PAIR = 2


def owner_column(place, mine, width):
    me = lax.axis_index("dom")
    z = me // PAIR
    y = me % PAIR
    low = z < 2
    stop = [
        jnp.where(low, 3, 0), jnp.where(low, 2, 1), jnp.where(low, 1 - z, 5 - z), z
    ][place]
    side = y if mine else 1 - y
    return pl.multiple_of((stop * PAIR + side) * width, width)


def put_mass(ref, mass):
    ngroup, hpad = mass.shape
    at = ref.shape[0] - ngroup
    ref[at:, 0:hpad] = mass
    ref[at:, hpad:] = jnp.zeros((ngroup, ref.shape[1] - hpad), F32)


def first_kernel(nstat, *refs):
    stats_refs = refs[:nstat]
    weight_ref, copies_ref, onehot_ref, post_ref, send_ref, mass_ref, loglik_ref = refs[nstat:]
    hpad = post_ref.shape[0] // 2
    ngroup = onehot_ref.shape[0]
    width = send_ref.shape[1]
    send = send_ref.shape[0] - ngroup
    mass = posterior(stats_refs, weight_ref, onehot_ref, post_ref, loglik_ref)
    sums = class_sums(post_ref, copies_ref, pl.ds(0, hpad), owner_column(0, False, width), width)
    send_ref[0:send, :] = sums[0:send]
    put_mass(send_ref, mass[0])
    put_mass(mass_ref, mass[1])


def second_kernel(post_ref, copies_ref, mass_ref, send_ref):
    hpad = post_ref.shape[0] // 2
    width = send_ref.shape[1]
    send = send_ref.shape[0] - mass_ref.shape[0]
    sums = class_sums(post_ref, copies_ref, pl.ds(hpad, hpad), owner_column(0, False, width), width)
    send_ref[0:send, :] = sums[0:send]
    send_ref[send:, :] = mass_ref[...]


def rest_kernel(post_ref, copies_ref, send_a_ref, mass_ref, *out_refs):
    hpad = post_ref.shape[0] // 2
    width = mass_ref.shape[1]
    chains = (out_refs[:7], out_refs[7:])
    send = chains[0][1].shape[0]
    for place in (1, 0, 2, 3):
        for mine in (False, True):
            if place == 0 and not mine:
                continue
            at = owner_column(place, mine, width)

            @pl.when(at >= 0)
            def _(at=at, place=place, mine=mine):
                sums = class_sums(post_ref, copies_ref, pl.ds(0, 2 * hpad), at, width)
                for index, refs in enumerate(chains):
                    ref = refs[0] if place == 0 else refs[2 * place - 1 + int(mine)]
                    ref[0:send, :] = sums[index * hpad : index * hpad + send]

    chains[0][0][send:, :] = send_a_ref[send:, :]
    chains[1][0][send:, :] = mass_ref[...]


def last_kernel(chain, classes, rots, images, *refs):
    (keep_ref, pair_ref, own_ref, line_ref, cross_ref, share_ref), refs = refs[:6], refs[6:]
    before, refs = (refs[:2], refs[2:]) if chain else (None, refs)
    new_ref, frac_ref, ratio_ref = refs
    send, width = keep_ref.shape
    mine = rots // 2
    z = lax.axis_index("dom") // PAIR
    end = (z == 0) | (z == LINE - 1)
    mass = jnp.where(end, line_ref[send:, :], own_ref[send:, :])
    den = lax.dot_general(
        mass, share_ref[...], (((0,), (0,)), ((), ())), precision=HI, preferred_element_type=F32
    )
    num = keep_ref[...] + pair_ref[...] + line_ref[0:send, :]
    num = num + jnp.where(end, 0.0, cross_ref[...])
    ratio_ref[0:send, :] = num / (den[0:send] + 1.0)
    ratio_ref[send:, :] = jnp.zeros((ratio_ref.shape[0] - send, width), F32)

    piece = 32
    per = 128 // piece
    kpad = round_up(classes, 8)
    lane = lax.broadcasted_iota(jnp.int32, (kpad, 128), 1)
    tiles = []
    for chunk in range(0, width, piece):
        base = chunk // 128 * 128
        parts = []
        for r0 in range(0, mine, per):
            acc = jnp.zeros((kpad, 128), F32)
            for u in range(min(per, mine - r0)):
                start = (r0 + u) * classes
                values = ratio_ref[start : start + kpad, base : base + 128]
                turn = (u * piece - (chunk - base)) % 128
                if turn:
                    values = pltpu.roll(values, turn, 1)
                acc = jnp.where((lane >= u * piece) & (lane < (u + 1) * piece), values, acc)
            parts.append(acc)
        tiles.append(jnp.concatenate(parts, axis=1))
    wide = piece * rots
    deep = tiles[0].shape[1]
    src = lax.broadcasted_iota(jnp.int32, (deep, wide), 0)
    dst = lax.broadcasted_iota(jnp.int32, (deep, wide), 1)
    src_r = src // piece
    perm = ((src - src_r * piece) * rots + src_r + chain * mine == dst) & (src_r < mine)
    moved = jnp.dot(
        thirds(jnp.concatenate(tiles, axis=0), 0), perm.astype(BF16), preferred_element_type=F32
    )
    count = len(tiles) * kpad
    moved = moved[0:count] + moved[count : 2 * count] + moved[2 * count :]
    for index in range(len(tiles)):
        columns = slice(index * wide, (index + 1) * wide)
        value = moved[index * kpad : index * kpad + classes, :]
        new_ref[:, columns] = value + before[0][:, columns] if before else value
    mrow = lax.broadcasted_iota(jnp.int32, (width, classes), 0)
    mcol = lax.broadcasted_iota(jnp.int32, (width, classes), 1)
    place = mrow.astype(F32)
    place = place - classes * jnp.floor((place + 0.5) * (1.0 / classes))
    member = ((place == mcol.astype(F32)) & (mrow < mine * classes)).astype(F32)
    share = jnp.dot(
        jnp.sum(mass, axis=0, keepdims=True), member, precision=HI, preferred_element_type=F32
    )
    if before:
        share = share + before[1][...]
        frac_ref[...] = (share / images).reshape(classes)
    else:
        frac_ref[...] = share


def line_path(stats, weight, copies, onehot, share, classes, rots, images):
    half = classes * rots // 2
    send = round_up(half, 8)
    ngroup, width = share.shape
    dom_n = lax.axis_size("dom")
    cls_n = lax.axis_size("cls")
    full = jax.ShapeDtypeStruct((send + ngroup, width), F32)
    body = jax.ShapeDtypeStruct((send, width), F32)
    mass_shape = jax.ShapeDtypeStruct((ngroup, width), F32)

    def first(*refs):
        first_kernel(len(stats), *refs)

    post, send_a, mass_b, loglik = pl.pallas_call(
        first,
        out_shape=(
            jax.ShapeDtypeStruct(weight.shape, BF16),
            full,
            mass_shape,
            jax.ShapeDtypeStruct(onehot.shape[1:], F32),
        ),
        in_specs=[VMEM] * (len(stats) + 3),
        out_specs=(VMEM,) * 4,
        compiler_params=PARAMS,
        name="first_sums",
    )(*stats, weight, copies, onehot)
    send_b = pl.pallas_call(
        second_kernel,
        out_shape=full,
        in_specs=[VMEM] * 3,
        out_specs=VMEM,
        compiler_params=PARAMS,
        name="second_sums",
    )(post, copies, mass_b)
    parts = pl.pallas_call(
        rest_kernel,
        out_shape=((full,) + (body,) * 6) * 2,
        in_specs=[VMEM] * 4,
        out_specs=(VMEM,) * 14,
        compiler_params=PARAMS,
        name="rest_sums",
    )(post, copies, send_a, mass_b)

    def along(pairs):
        return [(a * PAIR + y, b * PAIR + y) for a, b in pairs for y in range(PAIR)]

    across = [(d, d ^ 1) for d in range(dom_n)]
    outer = along([(0, 1), (1, 0), (2, 3), (3, 2)])
    facing = {0: 0, 1: 2, 2: 1, 3: 3}
    middle = [
        (
            (a * PAIR + y) * cls_n + c,
            (b * PAIR + y) * cls_n + (c if a != b else c ^ 1),
        )
        for a, b in facing.items()
        for y in range(PAIR)
        for c in range(cls_n)
    ]
    z = lax.axis_index("dom") // PAIR
    inner = (z != 0) & (z != LINE - 1)

    def swap(value):
        return lax.ppermute(value, "dom", across)

    def reduce_chain(send0, keep0, send1, keep1, send2, keep2, send3, keep3):
        pair0 = swap(send0)
        send1, pair0 = lax.optimization_barrier((send1, pair0))
        pair1 = swap(send1)
        send2, pair1 = lax.optimization_barrier((send2, pair1))
        pair2 = swap(send2)
        send3, pair2 = lax.optimization_barrier((send3, pair2))
        pair = swap(send3)
        sum0 = keep0 + pair0
        sum1 = keep1 + pair1
        sum2 = keep2 + pair2
        both0 = sum0 + lax.ppermute(sum0, "dom", outer)
        got1 = lax.ppermute(sum1, "dom", outer)
        got2 = lax.ppermute(both0, ("dom", "cls"), middle)
        to_ends = jnp.concatenate([sum2, both0[send:]], axis=0) + jnp.where(inner, got2, 0.0)
        line = lax.ppermute(to_ends, "dom", outer)
        cross = lax.ppermute(sum1 + got1, ("dom", "cls"), middle)
        return keep3, pair, to_ends, line, cross

    chain_a = reduce_chain(send_a, *parts[:7])
    chain_b = reduce_chain(send_b, *parts[7:])
    before = ()
    for chain, pieces in enumerate((chain_a, chain_b)):

        def last(*refs, chain=chain):
            last_kernel(chain, classes, rots, images, *refs)

        before = pl.pallas_call(
            last,
            out_shape=(
                jax.ShapeDtypeStruct((classes, width * rots), F32),
                jax.ShapeDtypeStruct((classes,) if chain else (1, classes), F32),
            ),
            in_specs=[VMEM] * (6 + len(before)),
            out_specs=(VMEM, VMEM),
            scratch_shapes=[pltpu.VMEM((send + 16, width), F32)],
            compiler_params=PARAMS,
            name="last_ratio",
        )(*pieces, share, *before)
    return before[0], loglik, before[1]


def plain_path(stats, weight, copies, onehot, ctf, inv_noise, classes, rots, images):
    rpad = weight.shape[0]
    hpad = rpad // 2
    half = classes * rots // 2
    ngroup, fpix = ctf.shape
    two_f = 2 * fpix
    dom_n = lax.axis_size("dom")
    width = two_f // dom_n
    nstat = len(stats)

    def sums(*refs):
        weight_ref, copies_ref, onehot_ref, num_ref, mass_ref, loglik_ref, post_ref = refs[nstat:]
        mass = posterior(refs[:nstat], weight_ref, onehot_ref, post_ref, loglik_ref)
        mass_ref[0] = mass[0]
        mass_ref[1] = mass[1]
        for at in range(0, two_f, 256):
            num_ref[:, at : at + 256] = class_sums(
                post_ref, copies_ref, pl.ds(0, rpad), at, 256
            )

    num, mass, loglik = pl.pallas_call(
        sums,
        out_shape=(
            jax.ShapeDtypeStruct((rpad, two_f), F32),
            jax.ShapeDtypeStruct((2, ngroup, hpad), F32),
            jax.ShapeDtypeStruct(onehot.shape[1:], F32),
        ),
        in_specs=[VMEM] * (len(stats) + 3),
        out_specs=(VMEM,) * 3,
        scratch_shapes=[pltpu.VMEM(weight.shape, BF16)],
        compiler_params=PARAMS,
        name="all_sums",
    )(*stats, weight, copies, onehot)
    mass = jnp.concatenate([mass[0, :, :half], mass[1, :, :half]], axis=1)
    mass = lax.psum(mass, "dom")
    num = jnp.concatenate([num[:half], num[hpad : hpad + half]], axis=0)
    num = lax.psum_scatter(num, "dom", scatter_dimension=1, tiled=True)
    c2w = ctf * ctf * inv_noise
    c2w_two = jnp.concatenate([c2w, c2w], axis=1)
    c2w_part = lax.dynamic_slice_in_dim(c2w_two, lax.axis_index("dom") * width, width, 1)
    den = jnp.einsum("gn,gq->nq", mass, c2w_part, precision=HI)
    ratio = (num / (den + 1.0)).reshape(rots, classes, width)
    new_refs = ratio.transpose(1, 2, 0).reshape(classes, width * rots)
    frac = jnp.sum(mass.reshape(ngroup, rots, classes), axis=(0, 1)) / images
    return new_refs, loglik, frac


def local(images, refs, ctf, inv_noise, log_prior, shifts, rot_prior, groups):
    classes, rots, two_f = refs.shape
    half = classes * rots // 2
    hpad = round_up(half, 16)
    count = images.shape[0]
    ngroup = ctf.shape[0]
    dom_n = lax.axis_size("dom")
    cls_n = lax.axis_size("cls")
    width = two_f // dom_n
    weight, copies, stat, onehot, share = estep(
        images, refs, ctf, inv_noise, log_prior, shifts, rot_prior, groups, 2 * hpad, width
    )
    stats = [stat] + [
        lax.ppermute(stat, "cls", [((c + ahead) % cls_n, c) for c in range(cls_n)])
        for ahead in range(1, cls_n)
    ]
    fits = (
        dom_n == LINE * PAIR
        and cls_n % 2 == 0
        and width % 128 == 0
        and hpad <= width
        and ngroup % 8 == 0
    )
    images_n = count * dom_n
    if fits:
        return line_path(stats, weight, copies, onehot, share, classes, rots, images_n)
    return plain_path(stats, weight, copies, onehot, ctf, inv_noise, classes, rots, images_n)


def solution(mesh):
    return jax.shard_map(
        local,
        mesh=mesh,
        in_specs=(
            P("dom", None),
            P("cls", None, None),
            P(),
            P(),
            P("cls"),
            P(),
            P("dom"),
            P("dom"),
        ),
        out_specs=(P("cls", "dom"), P("dom"), P("cls")),
        check_vma=False,
    )
```

time: 196 us -> 53.1 us (0.27)
  local copies, waits for them, and re-layouts: 75.3 us -> 0.01 us
  blocking collectives: 52.9 us -> 0 us
  starting transfers between devices: 0.04 us -> 24.5 us
  matrix products: 15.5 us -> 0 us
  waiting for transfers between devices: 28 us -> 13.6 us
  Pallas kernels: 0 us -> 13.7 us
  between operations: 14.3 us -> 0.8 us
  other arithmetic: 9.7 us -> 0.26 us
    reshape x4 -> x0, local copies, waits for them, and re-layouts: 50.2 us -> none  [the longest x1 49.8 us: local(): full.reshape(classes, two_f * rots)]
    psum x2 -> x0, blocking collectives: 44.5 us -> none  [the longest x1 38.6 us: local(): mass = lax.psum(local_mass, 'dom')]
    reduce_scatter x1 -> x0, waiting for transfers between devices: 27.9 us -> none  [local(): lax.psum_scatter(full.reshape(classes, two_f * rots), 'dom', scatter_dime...]
    ppermute x0 -> x21, starting transfers between devices: none -> 24.5 us  [the longest x8 8.98 us: swap(): return lax.ppermute(value, 'dom', across)]
    transpose x1 -> x0, local copies, waits for them, and re-layouts: 16.5 us -> none  [local(): jnp.einsum('nkr,nq->kqr', post_rows, rows, preferred_element_type=jnp.flo...]
    dot_general x7 -> x0, matrix products: 15.5 us -> none  [the longest x1 6.21 us: local(): jnp.einsum('nkr,nq->kqr', post_rows, rows, preferred_element_type=jnp.flo...]
    pallas_call x0 -> x6, Pallas kernels: none -> 13.7 us  [the longest x1 6.69 us: estep(): pl.pallas_call(estep_kernel, out_shape=(jax.ShapeDtypeStruct((rpad, nshif...]
    ppermute x0 -> x21, waiting for transfers between devices: none -> 13.6 us  [the longest x8 7.52 us: swap(): return lax.ppermute(value, 'dom', across)]
  transfers between devices with their start and end apart: 1 -> 21, of which waited for: 1 -> 12; matrix products, arithmetic and copies ran while one was open for 4% -> 1% of each run, Pallas kernels for 0% -> 8%
where the time goes in v1:
time: 53.1 us; the launch traced here: 53 us
  starting transfers between devices  24.5 us (46%)
  Pallas kernels  13.7 us (26%)
  waiting for transfers between devices  13.6 us (26%)
  between operations  0.8 us (2%)
    ppermute x8, starting transfers between devices, swap(): return lax.ppermute(value, 'dom', across)  8.98 us
    ppermute x8, waiting for transfers between devices, swap(): return lax.ppermute(value, 'dom', across)  7.52 us
    pallas_call x1, Pallas kernels, estep(): pl.pallas_call(estep_kernel, out_shape=(jax.ShapeDtypeStruct((rpad, nshif...  6.69 us
    ppermute x2, starting transfers between devices, reduce_chain(): line = lax.ppermute(to_ends, 'dom', outer)  4.66 us
    ppermute x2, starting transfers between devices, reduce_chain(): got1 = lax.ppermute(sum1, 'dom', outer)  3.95 us
    ppermute x2, starting transfers between devices, reduce_chain(): both0 = sum0 + lax.ppermute(sum0, 'dom', outer)  3.28 us
    ppermute x3, starting transfers between devices, local(): lax.ppermute(stat, 'cls', [((c + ahead) % cls_n, c) for c in range(cls_n)])  3.23 us
    pallas_call x2, Pallas kernels, line_path(): pl.pallas_call(last, out_shape=(jax.ShapeDtypeStruct((classes, width * ro...  3.14 us
  transfers between devices with their start and end apart: 21, of which 12 were waited for; matrix products, arithmetic and copies ran while one was open for 1% of the time, Pallas kernels for 8%

profile of v1, /device:TPU:0, one launch (start us, length us, event | category | flops | bytes accessed | tf_op | source)
XLA Modules:
  0.0 53.0 jit_solution(8090508753880670668)
XLA Ops:
  0.6 6.7 %estep.1 = (f32[320,1152]{1,0:T(8,128)S(1)}, bf16[1152,2048]{1,0:T(8,128)(2,1)S(1)}, f32[2,128]{1,0:T(2,128)S(1)}, f32[16,128]{1,0:T(8,128)S(1)}, f32[16,256]{1,0:T(8,128)S(1)}) custom-call(bf16[128,2048]{1,0:T(8,128)(2,1)} %images_hbm.1, bf16[12,25,2048]{2,1,0:T(8,128)(2,1)} %bitcast.2, f32[16,1024]{1,0:T(8,128)} %ctf_hbm.1, f32[16,1024]{1,0:T(8,128)} %inv_hbm.1, ...), custom_call_target="tpu_custom_call" | custom-call | tf_op jit(solution)/shard_map/estep/pallas_call | solution.py:178
  7.3 2.4 %collective-permute-start = (f32[2,128]{1,0:T(2,128)S(1)}, f32[2,128]{1,0:T(2,128)S(1)}, u32[]{:S(2)}, u32[]{:S(2)}) collective-permute-start(f32[2,128]{1,0:T(2,128)S(1)} %get-tuple-element.42.refs_0_), channel_id=1, source_target_pairs={{1,0},{2,1},{3,2},{0,3},{5,4},{6,5},{7,6},{4,7},{9,8},{10,9},{11,1... | collective-permute-start | bytes 3080 | tf_op jit(solution)/shard_map/ppermute | solution.py:556
  9.8 0.6 %collective-permute-start.1 = (f32[2,128]{1,0:T(2,128)S(1)}, f32[2,128]{1,0:T(2,128)S(1)}, u32[]{:S(2)}, u32[]{:S(2)}) collective-permute-start(f32[2,128]{1,0:T(2,128)S(1)} %get-tuple-element.42.refs_0_), channel_id=1, source_target_pairs={{2,0},{3,1},{0,2},{1,3},{6,4},{7,5},{4,6},{5,7},{10,8},{11,9},{8,1... | collective-permute-start | bytes 3080 | tf_op jit(solution)/shard_map/ppermute | solution.py:556
  10.4 0.2 collective-permute-start.2
  10.6 0.5 collective-permute-done.refs_1_
  11.1 2.3 %collective-permute-done.1.refs_2_ = f32[2,128]{1,0:T(2,128)S(1)} collective-permute-done((f32[2,128]{1,0:T(2,128)S(1)}, f32[2,128]{1,0:T(2,128)S(1)}, u32[]{:S(2)}, u32[]{:S(2)}) %collective-permute-start.1) | collective-permute-done | bytes 1056 | tf_op jit(solution)/shard_map/ppermute | solution.py:556
  13.3 0.1 collective-permute-done.2.refs_3_
  13.4 0.9 %first_sums.1 = (bf16[320,1152]{1,0:T(8,128)(2,1)S(1)}, f32[168,256]{1,0:T(8,128)S(1)}, f32[16,256]{1,0:T(8,128)S(1)}, f32[128]{0:T(128)}) custom-call(f32[2,128]{1,0:T(2,128)S(1)} %get-tuple-element.42.refs_0_, f32[2,128]{1,0:T(2,128)S(1)} %collective-permute-done.refs_1_, f32[2,128]{1,0:T(2,128)S(1)} %collective-permute-done.1.refs_2_, ...), custom_call_target="tpu_custom_call" | custom-call | tf_op jit(solution)/shard_map/first_sums/pallas_call | solution.py:403
  14.3 1.5 %collective-permute-start.12 = (f32[168,256]{1,0:T(8,128)S(1)}, f32[168,256]{1,0:T(8,128)S(1)}, u32[]{:S(2)}, u32[]{:S(2)}) collective-permute-start(f32[168,256]{1,0:T(8,128)S(1)} %get-tuple-element.47.send_a_ref), channel_id=1, source_target_pairs={{0,4},{4,0},{8,12},{12,8},{16,20},{20,16},{24,28},{28,24},{1,5},{5... | collective-permute-start | bytes 516104 | tf_op jit(solution)/shard_map/ppermute | solution.py:452
  15.8 0.3 second_sums.1
  16.1 0.6 %collective-permute-start.3 = (f32[168,256]{1,0:T(8,128)S(1)}, f32[168,256]{1,0:T(8,128)S(1)}, u32[]{:S(2)}, u32[]{:S(2)}) collective-permute-start(f32[168,256]{1,0:T(8,128)S(1)} %second_sums.1), channel_id=1, source_target_pairs={{0,4},{4,0},{8,12},{12,8},{16,20},{20,16},{24,28},{28,24},{1,5},{5... | collective-permute-start | bytes 516104 | tf_op jit(solution)/shard_map/ppermute | solution.py:452
  16.7 2.7 %rest_sums.1 = (f32[168,256]{1,0:T(8,128)S(1)}, f32[152,256]{1,0:T(8,128)S(1)}, f32[152,256]{1,0:T(8,128)S(1)}, f32[152,256]{1,0:T(8,128)S(1)}, f32[152,256]{1,0...) custom-call(bf16[320,1152]{1,0:T(8,128)(2,1)S(1)} %get-tuple-element, ...), custom_call_target="tpu_custom_call" | custom-call | tf_op jit(solution)/shard_map/rest_sums/pallas_call | solution.py:424
  19.4 2.2 %collective-permute-done.12 = f32[168,256]{1,0:T(8,128)S(1)} collective-permute-done((f32[168,256]{1,0:T(8,128)S(1)}, f32[168,256]{1,0:T(8,128)S(1)}, u32[]{:S(2)}, u32[]{:S(2)}) %collective-permute-start.12) | collective-permute-done | bytes 172064 | tf_op jit(solution)/shard_map/ppermute | solution.py:452
  21.6 1.6 %collective-permute-start.16 = (f32[168,256]{1,0:T(8,128)S(1)}, f32[168,256]{1,0:T(8,128)S(1)}, u32[]{:S(2)}, u32[]{:S(2)}) collective-permute-start(f32[168,256]{1,0:T(8,128)S(1)} %add.44), channel_id=1, source_target_pairs={{0,8},{4,12},{8,0},{12,4},{16,24},{20,28},{24,16},{28,20},{1,9},{5... | collective-permute-start | bytes 516104 | tf_op jit(solution)/shard_map/ppermute | solution.py:465
  23.3 0.2 collective-permute-done.3
  23.5 1.5 %collective-permute-start.4 = (f32[152,256]{1,0:T(8,128)S(1)}, f32[152,256]{1,0:T(8,128)S(1)}, u32[]{:S(2)}, u32[]{:S(2)}) collective-permute-start(f32[152,256]{1,0:T(8,128)S(1)} %get-tuple-element.53), channel_id=1, source_target_pairs={{0,4},{4,0},{8,12},{12,8},{16,20},{20,16},{24,28},{28,24},{1,5},{5... | collective-permute-start | bytes 466952 | tf_op jit(solution)/shard_map/ppermute | solution.py:452
  25.0 0.5 collective-permute-start.13
  25.6 1.6 %collective-permute-start.7 = (f32[168,256]{1,0:T(8,128)S(1)}, f32[168,256]{1,0:T(8,128)S(1)}, u32[]{:S(2)}, u32[]{:S(2)}) collective-permute-start(f32[168,256]{1,0:T(8,128)S(1)} %add.38), channel_id=1, source_target_pairs={{0,8},{4,12},{8,0},{12,4},{16,24},{20,28},{24,16},{28,20},{1,9},{5... | collective-permute-start | bytes 516104 | tf_op jit(solution)/shard_map/ppermute | solution.py:465
  27.2 1.1 %collective-permute-done.16 = f32[168,256]{1,0:T(8,128)S(1)} collective-permute-done((f32[168,256]{1,0:T(8,128)S(1)}, f32[168,256]{1,0:T(8,128)S(1)}, u32[]{:S(2)}, u32[]{:S(2)}) %collective-permute-start.16) | collective-permute-done | bytes 172064 | tf_op jit(solution)/shard_map/ppermute | solution.py:465
  28.3 0.1 collective-permute-start.17
  28.4 1.0 %collective-permute-done.4 = f32[152,256]{1,0:T(8,128)S(1)} collective-permute-done((f32[152,256]{1,0:T(8,128)S(1)}, f32[152,256]{1,0:T(8,128)S(1)}, u32[]{:S(2)}, u32[]{:S(2)}) %collective-permute-start.4) | collective-permute-done | bytes 155680 | tf_op jit(solution)/shard_map/ppermute | solution.py:452
  29.4 1.5 %collective-permute-start.5 = (f32[152,256]{1,0:T(8,128)S(1)}, f32[152,256]{1,0:T(8,128)S(1)}, u32[]{:S(2)}, u32[]{:S(2)}) collective-permute-start(f32[152,256]{1,0:T(8,128)S(1)} %get-tuple-element.54), channel_id=1, source_target_pairs={{0,4},{4,0},{8,12},{12,8},{16,20},{20,16},{24,28},{28,24},{1,5},{5... | collective-permute-start | bytes 466952 | tf_op jit(solution)/shard_map/ppermute | solution.py:452
  30.9 0.2 collective-permute-done.13
  31.1 1.5 %collective-permute-start.14 = (f32[152,256]{1,0:T(8,128)S(1)}, f32[152,256]{1,0:T(8,128)S(1)}, u32[]{:S(2)}, u32[]{:S(2)}) collective-permute-start(f32[152,256]{1,0:T(8,128)S(1)} %get-tuple-element.68), channel_id=1, source_target_pairs={{0,4},{4,0},{8,12},{12,8},{16,20},{20,16},{24,28},{28,24},{1,5},{5... | collective-permute-start | bytes 466952 | tf_op jit(solution)/shard_map/ppermute | solution.py:452
  32.6 3.9 %collective-permute-start.10 = (f32[152,256]{1,0:T(8,128)S(1)}, f32[152,256]{1,0:T(8,128)S(1)}, u32[]{:S(2)}, u32[]{:S(2)}) collective-permute-start(f32[152,256]{1,0:T(8,128)S(1)} %add.41), channel_id=1, source_target_pairs={{0,8},{4,12},{8,0},{12,4},{16,24},{20,28},{24,16},{28,20},{1,9},{5... | collective-permute-start | bytes 466952 | tf_op jit(solution)/shard_map/ppermute | solution.py:466
  36.5 0.0 collective-permute-done.7
  36.5 0.1 collective-permute-start.19
  36.6 0.0 collective-permute-done.5
  36.7 0.1 collective-permute-start.8
  36.7 1.4 %collective-permute-done.14 = f32[152,256]{1,0:T(8,128)S(1)} collective-permute-done((f32[152,256]{1,0:T(8,128)S(1)}, f32[152,256]{1,0:T(8,128)S(1)}, u32[]{:S(2)}, u32[]{:S(2)}) %collective-permute-start.14) | collective-permute-done | bytes 155680 | tf_op jit(solution)/shard_map/ppermute | solution.py:452
  38.2 1.5 %collective-permute-start.15 = (f32[152,256]{1,0:T(8,128)S(1)}, f32[152,256]{1,0:T(8,128)S(1)}, u32[]{:S(2)}, u32[]{:S(2)}) collective-permute-start(f32[152,256]{1,0:T(8,128)S(1)} %get-tuple-element.69), channel_id=1, source_target_pairs={{0,4},{4,0},{8,12},{12,8},{16,20},{20,16},{24,28},{28,24},{1,5},{5... | collective-permute-start | bytes 466952 | tf_op jit(solution)/shard_map/ppermute | solution.py:452
  39.7 0.0 collective-permute-done.17
  39.8 2.6 %collective-permute-start.18 = (f32[168,256]{1,0:T(8,128)S(1)}, f32[168,256]{1,0:T(8,128)S(1)}, u32[]{:S(2)}, u32[]{:S(2)}) collective-permute-start(f32[168,256]{1,0:T(8,128)S(1)} %maximum_add_fusion.1.refs_2_), channel_id=1, source_target_pairs={{0,8},{4,12},{8,0},{12,4},{16,24},{20,28},{24,16},{28,20},{1,9},{5... | collective-permute-start | bytes 516104 | tf_op jit(solution)/shard_map/ppermute | solution.py:469
  42.4 0.0 collective-permute-done.8
  42.4 2.0 %collective-permute-start.9 = (f32[168,256]{1,0:T(8,128)S(1)}, f32[168,256]{1,0:T(8,128)S(1)}, u32[]{:S(2)}, u32[]{:S(2)}) collective-permute-start(f32[168,256]{1,0:T(8,128)S(1)} %maximum_add_fusion.refs_2_), channel_id=1, source_target_pairs={{0,8},{4,12},{8,0},{12,4},{16,24},{20,28},{24,16},{28,20},{1,9},{5... | collective-permute-start | bytes 516104 | tf_op jit(solution)/shard_map/ppermute | solution.py:469
  44.5 0.0 collective-permute-done.19
  44.5 0.1 collective-permute-start.20
  44.6 0.0 collective-permute-done.10
  44.6 0.3 collective-permute-start.6
  45.0 0.0 collective-permute-done.15.refs_1_
  45.0 0.2 collective-permute-start.11
  45.2 0.8 %collective-permute-done.20.refs_4_ = f32[152,256]{1,0:T(8,128)S(1)} collective-permute-done((f32[152,256]{1,0:T(8,128)S(1)}, f32[152,256]{1,0:T(8,128)S(1)}, u32[]{:S(2)}, u32[]{:S(2)}) %collective-permute-start.20) | collective-permute-done | bytes 155680 | tf_op jit(solution)/shard_map/ppermute | solution.py:470
  46.0 1.4 %collective-permute-done.18.refs_3_ = f32[168,256]{1,0:T(8,128)S(1)} collective-permute-done((f32[168,256]{1,0:T(8,128)S(1)}, f32[168,256]{1,0:T(8,128)S(1)}, u32[]{:S(2)}, u32[]{:S(2)}) %collective-permute-start.18) | collective-permute-done | bytes 172064 | tf_op jit(solution)/shard_map/ppermute | solution.py:469
  47.4 1.2 %last_ratio.2 = (f32[25,3072]{1,0:T(8,128)S(1)}, f32[1,25]{1,0:T(1,128)S(1)}) custom-call(f32[152,256]{1,0:T(8,128)S(1)} %get-tuple-element.63.refs_0_, f32[152,256]{1,0:T(8,128)S(1)} %collective-permute-done.15.refs_1_, f32[168,256]{1,0:T(8,128)S(1)} %maximum_add_fusion.1.refs_2_, f32[168,256]{1,0:T(8,128)S(1)} %collective-permute-done.18.refs_3_, ...), custom_call_target="tpu_custom_call" | custom-call | tf_op jit(solution)/shard_map/last_ratio/pallas_call | solution.py:481
  48.5 2.5 %collective-permute-done.6.refs_1_ = f32[152,256]{1,0:T(8,128)S(1)} collective-permute-done((f32[152,256]{1,0:T(8,128)S(1)}, f32[152,256]{1,0:T(8,128)S(1)}, u32[]{:S(2)}, u32[]{:S(2)}) %collective-permute-start.6) | collective-permute-done | bytes 155680 | tf_op jit(solution)/shard_map/ppermute | solution.py:452
  51.0 0.0 collective-permute-done.11.refs_4_
  51.0 0.0 collective-permute-done.9.refs_3_
  51.0 2.0 %last_ratio.3 = (f32[25,3072]{1,0:T(8,128)}, f32[25]{0:T(128)}) custom-call(f32[152,256]{1,0:T(8,128)S(1)} %get-tuple-element.49.refs_0_, f32[152,256]{1,0:T(8,128)S(1)} %collective-permute-done.6.refs_1_, f32[168,256]{1,0:T(8,128)S(1)} %maximum_add_fusion.refs_2_, f32[168,256]{1,0:T(8,128)S(1)} %collective-permute-done.9.refs_3_, ...), custom_call_target="tpu_custom_call" | custom-call | tf_op jit(solution)/shard_map/last_ratio/pallas_call | solution.py:481
  (14 shorter events, 0.3 us)
Async XLA Ops:
  7.3 3.7 %collective-permute-start = (f32[2,128]{1,0:T(2,128)S(1)}, f32[2,128]{1,0:T(2,128)S(1)}, u32[]{:S(2)}, u32[]{:S(2)}) collective-permute-start(f32[2,128]{1,0:T(2,128)S(1)} %get-tuple-element.42.refs_0_), channel_id=1, source_target_pairs={{1,0},{2,1},{3,2},{0,3},{5,4},{6,5},{7,6},{4,7},{9,8},{10,9},{11,1... | collective-permute-start | bytes 3080 | tf_op jit(solution)/shard_map/ppermute | solution.py:556
  9.8 3.6 %collective-permute-start.1 = (f32[2,128]{1,0:T(2,128)S(1)}, f32[2,128]{1,0:T(2,128)S(1)}, u32[]{:S(2)}, u32[]{:S(2)}) collective-permute-start(f32[2,128]{1,0:T(2,128)S(1)} %get-tuple-element.42.refs_0_), channel_id=1, source_target_pairs={{2,0},{3,1},{0,2},{1,3},{6,4},{7,5},{4,6},{5,7},{10,8},{11,9},{8,1... | collective-permute-start | bytes 3080 | tf_op jit(solution)/shard_map/ppermute | solution.py:556
  10.4 3.0 %collective-permute-start.2 = (f32[2,128]{1,0:T(2,128)S(1)}, f32[2,128]{1,0:T(2,128)S(1)}, u32[]{:S(2)}, u32[]{:S(2)}) collective-permute-start(f32[2,128]{1,0:T(2,128)S(1)} %get-tuple-element.42.refs_0_), channel_id=1, source_target_pairs={{3,0},{0,1},{1,2},{2,3},{7,4},{4,5},{5,6},{6,7},{11,8},{8,9},{9,10... | collective-permute-start | bytes 3080 | tf_op jit(solution)/shard_map/ppermute | solution.py:556
  14.3 7.3 %collective-permute-start.12 = (f32[168,256]{1,0:T(8,128)S(1)}, f32[168,256]{1,0:T(8,128)S(1)}, u32[]{:S(2)}, u32[]{:S(2)}) collective-permute-start(f32[168,256]{1,0:T(8,128)S(1)} %get-tuple-element.47.send_a_ref), channel_id=1, source_target_pairs={{0,4},{4,0},{8,12},{12,8},{16,20},{20,16},{24,28},{28,24},{1,5},{5... | collective-permute-start | bytes 516104 | tf_op jit(solution)/shard_map/ppermute | solution.py:452
  16.1 7.4 %collective-permute-start.3 = (f32[168,256]{1,0:T(8,128)S(1)}, f32[168,256]{1,0:T(8,128)S(1)}, u32[]{:S(2)}, u32[]{:S(2)}) collective-permute-start(f32[168,256]{1,0:T(8,128)S(1)} %second_sums.1), channel_id=1, source_target_pairs={{0,4},{4,0},{8,12},{12,8},{16,20},{20,16},{24,28},{28,24},{1,5},{5... | collective-permute-start | bytes 516104 | tf_op jit(solution)/shard_map/ppermute | solution.py:452
  21.6 6.7 %collective-permute-start.16 = (f32[168,256]{1,0:T(8,128)S(1)}, f32[168,256]{1,0:T(8,128)S(1)}, u32[]{:S(2)}, u32[]{:S(2)}) collective-permute-start(f32[168,256]{1,0:T(8,128)S(1)} %add.44), channel_id=1, source_target_pairs={{0,8},{4,12},{8,0},{12,4},{16,24},{20,28},{24,16},{28,20},{1,9},{5... | collective-permute-start | bytes 516104 | tf_op jit(solution)/shard_map/ppermute | solution.py:465
  23.5 5.9 %collective-permute-start.4 = (f32[152,256]{1,0:T(8,128)S(1)}, f32[152,256]{1,0:T(8,128)S(1)}, u32[]{:S(2)}, u32[]{:S(2)}) collective-permute-start(f32[152,256]{1,0:T(8,128)S(1)} %get-tuple-element.53), channel_id=1, source_target_pairs={{0,4},{4,0},{8,12},{12,8},{16,20},{20,16},{24,28},{28,24},{1,5},{5... | collective-permute-start | bytes 466952 | tf_op jit(solution)/shard_map/ppermute | solution.py:452
  25.0 6.1 %collective-permute-start.13 = (f32[152,256]{1,0:T(8,128)S(1)}, f32[152,256]{1,0:T(8,128)S(1)}, u32[]{:S(2)}, u32[]{:S(2)}) collective-permute-start(f32[152,256]{1,0:T(8,128)S(1)} %get-tuple-element.67), channel_id=1, source_target_pairs={{0,4},{4,0},{8,12},{12,8},{16,20},{20,16},{24,28},{28,24},{1,5},{5... | collective-permute-start | bytes 466952 | tf_op jit(solution)/shard_map/ppermute | solution.py:452
  25.6 11.0 %collective-permute-start.7 = (f32[168,256]{1,0:T(8,128)S(1)}, f32[168,256]{1,0:T(8,128)S(1)}, u32[]{:S(2)}, u32[]{:S(2)}) collective-permute-start(f32[168,256]{1,0:T(8,128)S(1)} %add.38), channel_id=1, source_target_pairs={{0,8},{4,12},{8,0},{12,4},{16,24},{20,28},{24,16},{28,20},{1,9},{5... | collective-permute-start | bytes 516104 | tf_op jit(solution)/shard_map/ppermute | solution.py:465
  28.3 11.4 %collective-permute-start.17 = (f32[168,256]{1,0:T(8,128)S(1)}, f32[168,256]{1,0:T(8,128)S(1)}, u32[]{:S(2)}, u32[]{:S(2)}) collective-permute-start(f32[168,256]{1,0:T(8,128)S(1)} %add.45), channel_id=1, source_target_pairs={{0,1},{1,0},{2,3},{3,2},{4,5},{5,4},{6,7},{7,6},{8,16},{9,17},{10,... | collective-permute-start | bytes 516104 | tf_op jit(solution)/shard_map/ppermute | solution.py:467
  29.4 7.2 %collective-permute-start.5 = (f32[152,256]{1,0:T(8,128)S(1)}, f32[152,256]{1,0:T(8,128)S(1)}, u32[]{:S(2)}, u32[]{:S(2)}) collective-permute-start(f32[152,256]{1,0:T(8,128)S(1)} %get-tuple-element.54), channel_id=1, source_target_pairs={{0,4},{4,0},{8,12},{12,8},{16,20},{20,16},{24,28},{28,24},{1,5},{5... | collective-permute-start | bytes 466952 | tf_op jit(solution)/shard_map/ppermute | solution.py:452
  31.1 7.1 %collective-permute-start.14 = (f32[152,256]{1,0:T(8,128)S(1)}, f32[152,256]{1,0:T(8,128)S(1)}, u32[]{:S(2)}, u32[]{:S(2)}) collective-permute-start(f32[152,256]{1,0:T(8,128)S(1)} %get-tuple-element.68), channel_id=1, source_target_pairs={{0,4},{4,0},{8,12},{12,8},{16,20},{20,16},{24,28},{28,24},{1,5},{5... | collective-permute-start | bytes 466952 | tf_op jit(solution)/shard_map/ppermute | solution.py:452
  32.6 12.0 %collective-permute-start.10 = (f32[152,256]{1,0:T(8,128)S(1)}, f32[152,256]{1,0:T(8,128)S(1)}, u32[]{:S(2)}, u32[]{:S(2)}) collective-permute-start(f32[152,256]{1,0:T(8,128)S(1)} %add.41), channel_id=1, source_target_pairs={{0,8},{4,12},{8,0},{12,4},{16,24},{20,28},{24,16},{28,20},{1,9},{5... | collective-permute-start | bytes 466952 | tf_op jit(solution)/shard_map/ppermute | solution.py:466
  36.5 8.0 %collective-permute-start.19 = (f32[152,256]{1,0:T(8,128)S(1)}, f32[152,256]{1,0:T(8,128)S(1)}, u32[]{:S(2)}, u32[]{:S(2)}) collective-permute-start(f32[152,256]{1,0:T(8,128)S(1)} %add.47), channel_id=1, source_target_pairs={{0,8},{4,12},{8,0},{12,4},{16,24},{20,28},{24,16},{28,20},{1,9},{5... | collective-permute-start | bytes 466952 | tf_op jit(solution)/shard_map/ppermute | solution.py:466
  36.7 5.7 %collective-permute-start.8 = (f32[168,256]{1,0:T(8,128)S(1)}, f32[168,256]{1,0:T(8,128)S(1)}, u32[]{:S(2)}, u32[]{:S(2)}) collective-permute-start(f32[168,256]{1,0:T(8,128)S(1)} %add.39), channel_id=1, source_target_pairs={{0,1},{1,0},{2,3},{3,2},{4,5},{5,4},{6,7},{7,6},{8,16},{9,17},{10,... | collective-permute-start | bytes 516104 | tf_op jit(solution)/shard_map/ppermute | solution.py:467
  38.2 6.8 %collective-permute-start.15 = (f32[152,256]{1,0:T(8,128)S(1)}, f32[152,256]{1,0:T(8,128)S(1)}, u32[]{:S(2)}, u32[]{:S(2)}) collective-permute-start(f32[152,256]{1,0:T(8,128)S(1)} %get-tuple-element.69), channel_id=1, source_target_pairs={{0,4},{4,0},{8,12},{12,8},{16,20},{20,16},{24,28},{28,24},{1,5},{5... | collective-permute-start | bytes 466952 | tf_op jit(solution)/shard_map/ppermute | solution.py:452
  39.8 7.6 %collective-permute-start.18 = (f32[168,256]{1,0:T(8,128)S(1)}, f32[168,256]{1,0:T(8,128)S(1)}, u32[]{:S(2)}, u32[]{:S(2)}) collective-permute-start(f32[168,256]{1,0:T(8,128)S(1)} %maximum_add_fusion.1.refs_2_), channel_id=1, source_target_pairs={{0,8},{4,12},{8,0},{12,4},{16,24},{20,28},{24,16},{28,20},{1,9},{5... | collective-permute-start | bytes 516104 | tf_op jit(solution)/shard_map/ppermute | solution.py:469
  42.4 8.6 %collective-permute-start.9 = (f32[168,256]{1,0:T(8,128)S(1)}, f32[168,256]{1,0:T(8,128)S(1)}, u32[]{:S(2)}, u32[]{:S(2)}) collective-permute-start(f32[168,256]{1,0:T(8,128)S(1)} %maximum_add_fusion.refs_2_), channel_id=1, source_target_pairs={{0,8},{4,12},{8,0},{12,4},{16,24},{20,28},{24,16},{28,20},{1,9},{5... | collective-permute-start | bytes 516104 | tf_op jit(solution)/shard_map/ppermute | solution.py:469
  44.5 1.4 %collective-permute-start.20 = (f32[152,256]{1,0:T(8,128)S(1)}, f32[152,256]{1,0:T(8,128)S(1)}, u32[]{:S(2)}, u32[]{:S(2)}) collective-permute-start(f32[152,256]{1,0:T(8,128)S(1)} %add.48), channel_id=1, source_target_pairs={{0,1},{1,0},{2,3},{3,2},{4,5},{5,4},{6,7},{7,6},{8,16},{9,17},{10,... | collective-permute-start | bytes 466952 | tf_op jit(solution)/shard_map/ppermute | solution.py:470
  44.6 6.4 %collective-permute-start.6 = (f32[152,256]{1,0:T(8,128)S(1)}, f32[152,256]{1,0:T(8,128)S(1)}, u32[]{:S(2)}, u32[]{:S(2)}) collective-permute-start(f32[152,256]{1,0:T(8,128)S(1)} %get-tuple-element.55), channel_id=1, source_target_pairs={{0,4},{4,0},{8,12},{12,8},{16,20},{20,16},{24,28},{28,24},{1,5},{5... | collective-permute-start | bytes 466952 | tf_op jit(solution)/shard_map/ppermute | solution.py:452
  45.0 6.1 %collective-permute-start.11 = (f32[152,256]{1,0:T(8,128)S(1)}, f32[152,256]{1,0:T(8,128)S(1)}, u32[]{:S(2)}, u32[]{:S(2)}) collective-permute-start(f32[152,256]{1,0:T(8,128)S(1)} %add.42), channel_id=1, source_target_pairs={{0,1},{1,0},{2,3},{3,2},{4,5},{5,4},{6,7},{7,6},{8,16},{9,17},{10,... | collective-permute-start | bytes 466952 | tf_op jit(solution)/shard_map/ppermute | solution.py:470

commit v2 on v1

--- a/solution.py
+++ b/solution.py
@@ -221,7 +221,7 @@
     for place in range(parts):
         value = stats[0]
         for ahead in range(1, parts):
-            value = jnp.where(lax.rem(me + ahead, parts) == place, stats[ahead], value)
+            value = jnp.where(me ^ ahead == place, stats[ahead], value)
         ordered.append(value)
     peak = ordered[0][0:1]
     for value in ordered[1:]:
@@ -255,6 +255,8 @@
 
 LINE = 4
 PAIR = 2
+SLOW = 4_000_000_000
+QUICK = 1000
 
 
 def owner_column(place, mine, width):
@@ -302,7 +304,7 @@
 def rest_kernel(post_ref, copies_ref, send_a_ref, mass_ref, *out_refs):
     hpad = post_ref.shape[0] // 2
     width = mass_ref.shape[1]
-    chains = (out_refs[:7], out_refs[7:])
+    chains = (out_refs[:6], out_refs[6:12])
     send = chains[0][1].shape[0]
     for place in (1, 0, 2, 3):
         for mine in (False, True):
@@ -314,8 +316,12 @@
             def _(at=at, place=place, mine=mine):
                 sums = class_sums(post_ref, copies_ref, pl.ds(0, 2 * hpad), at, width)
                 for index, refs in enumerate(chains):
-                    ref = refs[0] if place == 0 else refs[2 * place - 1 + int(mine)]
-                    ref[0:send, :] = sums[index * hpad : index * hpad + send]
+                    value = sums[index * hpad : index * hpad + send]
+                    if place == 3 and not mine:
+                        out_refs[12][index * send : (index + 1) * send, :] = value
+                    else:
+                        slot = (0, 1 + int(mine), 3 + int(mine), 5)[place]
+                        refs[slot][0:send, :] = value
 
     chains[0][0][send:, :] = send_a_ref[send:, :]
     chains[1][0][send:, :] = mass_ref[...]
@@ -333,7 +339,7 @@
     den = lax.dot_general(
         mass, share_ref[...], (((0,), (0,)), ((), ())), precision=HI, preferred_element_type=F32
     )
-    num = keep_ref[...] + pair_ref[...] + line_ref[0:send, :]
+    num = keep_ref[...] + pair_ref[chain * send : (chain + 1) * send, :] + line_ref[0:send, :]
     num = num + jnp.where(end, 0.0, cross_ref[...])
     ratio_ref[0:send, :] = num / (den[0:send] + 1.0)
     ratio_ref[send:, :] = jnp.zeros((ratio_ref.shape[0] - send, width), F32)
@@ -343,18 +349,21 @@
     kpad = round_up(classes, 8)
     lane = lax.broadcasted_iota(jnp.int32, (kpad, 128), 1)
     tiles = []
+    values = [
+        [ratio_ref[r * classes : r * classes + kpad, base : base + 128] for r in range(mine)]
+        for base in range(0, width, 128)
+    ]
     for chunk in range(0, width, piece):
         base = chunk // 128 * 128
         parts = []
         for r0 in range(0, mine, per):
             acc = jnp.zeros((kpad, 128), F32)
             for u in range(min(per, mine - r0)):
-                start = (r0 + u) * classes
-                values = ratio_ref[start : start + kpad, base : base + 128]
+                turned = values[base // 128][r0 + u]
                 turn = (u * piece - (chunk - base)) % 128
                 if turn:
-                    values = pltpu.roll(values, turn, 1)
-                acc = jnp.where((lane >= u * piece) & (lane < (u + 1) * piece), values, acc)
+                    turned = pltpu.roll(turned, turn, 1)
+                acc = jnp.where((lane >= u * piece) & (lane < (u + 1) * piece), turned, acc)
             parts.append(acc)
         tiles.append(jnp.concatenate(parts, axis=1))
     wide = piece * rots
@@ -423,9 +432,9 @@
     )(post, copies, mass_b)
     parts = pl.pallas_call(
         rest_kernel,
-        out_shape=((full,) + (body,) * 6) * 2,
+        out_shape=((full,) + (body,) * 5) * 2 + (jax.ShapeDtypeStruct((2 * send, width), F32),),
         in_specs=[VMEM] * 4,
-        out_specs=(VMEM,) * 14,
+        out_specs=(VMEM,) * 13,
         compiler_params=PARAMS,
         name="rest_sums",
     )(post, copies, send_a, mass_b)
@@ -445,35 +454,63 @@
         for y in range(PAIR)
         for c in range(cls_n)
     ]
-    z = lax.axis_index("dom") // PAIR
-    inner = (z != 0) & (z != LINE - 1)
 
     def swap(value):
         return lax.ppermute(value, "dom", across)
 
-    def reduce_chain(send0, keep0, send1, keep1, send2, keep2, send3, keep3):
+    def join(kernel, cost, out_shape, *values):
+        return pl.pallas_call(
+            kernel,
+            out_shape=out_shape,
+            in_specs=[VMEM] * len(values),
+            out_specs=(VMEM,) * len(out_shape),
+            compiler_params=PARAMS,
+            cost_estimate=pl.CostEstimate(flops=cost, bytes_accessed=0, transcendentals=0),
+            name="join",
+        )(*values)
+
+    def add2(left, right, out):
+        out[...] = left[...] + right[...]
+
+    def join1(keep1, pair1, sum0, got0, sum1, both0):
+        sum1[...] = keep1[...] + pair1[...]
+        both0[...] = sum0[...] + got0[...]
+
+    def join2(keep2, pair2, sum1, got1, both0, got2, to_ends, to_middle):
+        to_middle[...] = sum1[...] + got1[...]
+        z = lax.axis_index("dom") // PAIR
+        inner = (z != 0) & (z != LINE - 1)
+        more = jnp.where(inner, got2[...], 0.0)
+        to_ends[0:send, :] = keep2[...] + pair2[...] + more[0:send]
+        to_ends[send:, :] = both0[send:, :] + more[send:]
+
+
+    def reduce_chain(send0, keep0, send1, keep1, send2, keep2):
         pair0 = swap(send0)
-        send1, pair0 = lax.optimization_barrier((send1, pair0))
+        (sum0,) = join(add2, QUICK, (full,), keep0, pair0)
+        send1, sum0 = lax.optimization_barrier((send1, sum0))
         pair1 = swap(send1)
-        send2, pair1 = lax.optimization_barrier((send2, pair1))
+        got0 = lax.ppermute(sum0, "dom", outer)
+        sum1, both0 = join(join1, SLOW, (body, full), keep1, pair1, sum0, got0)
+        send2, sum1, both0 = lax.optimization_barrier((send2, sum1, both0))
         pair2 = swap(send2)
-        send3, pair2 = lax.optimization_barrier((send3, pair2))
-        pair = swap(send3)
-        sum0 = keep0 + pair0
-        sum1 = keep1 + pair1
-        sum2 = keep2 + pair2
-        both0 = sum0 + lax.ppermute(sum0, "dom", outer)
         got1 = lax.ppermute(sum1, "dom", outer)
         got2 = lax.ppermute(both0, ("dom", "cls"), middle)
-        to_ends = jnp.concatenate([sum2, both0[send:]], axis=0) + jnp.where(inner, got2, 0.0)
+        to_ends, to_middle = join(
+            join2, SLOW, (full, body), keep2, pair2, sum1, got1, both0, got2
+        )
         line = lax.ppermute(to_ends, "dom", outer)
-        cross = lax.ppermute(sum1 + got1, ("dom", "cls"), middle)
-        return keep3, pair, to_ends, line, cross
-
-    chain_a = reduce_chain(send_a, *parts[:7])
-    chain_b = reduce_chain(send_b, *parts[7:])
+        cross = lax.ppermute(to_middle, ("dom", "cls"), middle)
+        return pair2, to_ends, line, cross
+
+    chain_a = reduce_chain(send_a, *parts[:5])
+    chain_b = reduce_chain(send_b, *parts[6:11])
+    send3, _ = lax.optimization_barrier((parts[12], chain_a[0]))
+    pair3 = swap(send3)
+    pieces_a = (parts[5], pair3) + chain_a[1:]
+    pieces_b = (parts[11], pair3) + chain_b[1:]
     before = ()
-    for chain, pieces in enumerate((chain_a, chain_b)):
+    for chain, pieces in enumerate((pieces_a, pieces_b)):
 
         def last(*refs, chain=chain):
             last_kernel(chain, classes, rots, images, *refs)
@@ -488,6 +525,7 @@
             out_specs=(VMEM, VMEM),
             scratch_shapes=[pltpu.VMEM((send + 16, width), F32)],
             compiler_params=PARAMS,
+            cost_estimate=pl.CostEstimate(flops=QUICK, bytes_accessed=0, transcendentals=0),
             name="last_ratio",
         )(*pieces, share, *before)
     return before[0], loglik, before[1]
@@ -552,9 +590,11 @@
     weight, copies, stat, onehot, share = estep(
         images, refs, ctf, inv_noise, log_prior, shifts, rot_prior, groups, 2 * hpad, width
     )
+    if cls_n & (cls_n - 1):
+        raise ValueError("cls size")
     stats = [stat] + [
-        lax.ppermute(stat, "cls", [((c + ahead) % cls_n, c) for c in range(cls_n)])
-        for ahead in range(1, cls_n)
+        lax.ppermute(stat, "cls", [(c, c ^ other) for c in range(cls_n)])
+        for other in range(1, cls_n)
     ]
     fits = (
         dom_n == LINE * PAIR

time: 53.1 us -> 50 us (0.942)
  waiting for transfers between devices: 13.6 us -> 10.6 us
    ppermute x8 -> x7, waiting for transfers between devices: 7.52 us -> 3.24 us  [swap(): return lax.ppermute(value, 'dom', across)]
    ppermute x2, waiting for transfers between devices: 1.4 us -> 2.46 us  [reduce_chain(): line = lax.ppermute(to_ends, 'dom', outer)]
    pallas_call x1 -> x7, Pallas kernels: 2.71 us -> 2.93 us  [the longest x1 2.7 us: line_path(): pl.pallas_call(rest_kernel, out_shape=((full,) + (body,) * 5) * 2 + (jax....]
    ppermute x8 -> x7, starting transfers between devices: 8.98 us -> 8.9 us  [swap(): return lax.ppermute(value, 'dom', across)]
  transfers between devices with their start and end apart: 21 -> 20, of which waited for: 12 -> 10; matrix products, arithmetic and copies ran while one was open for 1% -> 0% of each run, Pallas kernels for 8% -> 9%
where the time goes in v2:
time: 50 us; the launch traced here: 49.8 us
  starting transfers between devices  24.6 us (49%)
  Pallas kernels  13.9 us (28%)
  waiting for transfers between devices  10.6 us (21%)
  between operations  0.71 us (1%)
    ppermute x7, starting transfers between devices, swap(): return lax.ppermute(value, 'dom', across)  8.9 us
    pallas_call x1, Pallas kernels, estep(): pl.pallas_call(estep_kernel, out_shape=(jax.ShapeDtypeStruct((rpad, nshif...  6.69 us
    ppermute x2, starting transfers between devices, reduce_chain(): line = lax.ppermute(to_ends, 'dom', outer)  4.87 us
    ppermute x2, starting transfers between devices, reduce_chain(): got0 = lax.ppermute(sum0, 'dom', outer)  3.69 us
    ppermute x2, starting transfers between devices, reduce_chain(): got1 = lax.ppermute(sum1, 'dom', outer)  3.46 us
    ppermute x7, waiting for transfers between devices, swap(): return lax.ppermute(value, 'dom', across)  3.24 us
    pallas_call x2, Pallas kernels, line_path(): pl.pallas_call(last, out_shape=(jax.ShapeDtypeStruct((classes, width * ro...  3.13 us
    ppermute x3, starting transfers between devices, local(): lax.ppermute(stat, 'cls', [(c, c ^ other) for c in range(cls_n)])  3.12 us
  transfers between devices with their start and end apart: 20, of which 10 were waited for; matrix products, arithmetic and copies ran while one was open for 0% of the time, Pallas kernels for 9%

profile of v2, /device:TPU:0, one launch (start us, length us, event | category | flops | bytes accessed | tf_op | source)
XLA Modules:
  0.0 49.8 jit_solution(1621363491242536134)
XLA Ops:
  0.6 6.7 %estep.1 = (f32[320,1152]{1,0:T(8,128)S(1)}, bf16[1152,2048]{1,0:T(8,128)(2,1)S(1)}, f32[2,128]{1,0:T(2,128)S(1)}, f32[16,128]{1,0:T(8,128)S(1)}, f32[16,256]{1,0:T(8,128)S(1)}) custom-call(bf16[128,2048]{1,0:T(8,128)(2,1)} %images_hbm.1, bf16[12,25,2048]{2,1,0:T(8,128)(2,1)} %bitcast.2, f32[16,1024]{1,0:T(8,128)} %ctf_hbm.1, f32[16,1024]{1,0:T(8,128)} %inv_hbm.1, ...), custom_call_target="tpu_custom_call" | custom-call | tf_op jit(solution)/shard_map/estep/pallas_call | solution.py:178
  7.3 2.4 %collective-permute-start.2 = (f32[2,128]{1,0:T(2,128)S(1)}, f32[2,128]{1,0:T(2,128)S(1)}, u32[]{:S(2)}, u32[]{:S(2)}) collective-permute-start(f32[2,128]{1,0:T(2,128)S(1)} %get-tuple-element.48.refs_0_), channel_id=1, source_target_pairs={{0,3},{1,2},{2,1},{3,0},{4,7},{5,6},{6,5},{7,4},{8,11},{9,10},{10,... | collective-permute-start | bytes 3080 | tf_op jit(solution)/shard_map/ppermute | solution.py:596
  9.8 0.6 %collective-permute-start.1 = (f32[2,128]{1,0:T(2,128)S(1)}, f32[2,128]{1,0:T(2,128)S(1)}, u32[]{:S(2)}, u32[]{:S(2)}) collective-permute-start(f32[2,128]{1,0:T(2,128)S(1)} %get-tuple-element.48.refs_0_), channel_id=1, source_target_pairs={{0,2},{1,3},{2,0},{3,1},{4,6},{5,7},{6,4},{7,5},{8,10},{9,11},{10,... | collective-permute-start | bytes 3080 | tf_op jit(solution)/shard_map/ppermute | solution.py:596
  10.4 0.0 collective-permute-start
  10.5 0.6 %collective-permute-done.2.refs_3_ = f32[2,128]{1,0:T(2,128)S(1)} collective-permute-done((f32[2,128]{1,0:T(2,128)S(1)}, f32[2,128]{1,0:T(2,128)S(1)}, u32[]{:S(2)}, u32[]{:S(2)}) %collective-permute-start.2) | collective-permute-done | bytes 1056 | tf_op jit(solution)/shard_map/ppermute | solution.py:596
  11.1 2.3 %collective-permute-done.1.refs_2_ = f32[2,128]{1,0:T(2,128)S(1)} collective-permute-done((f32[2,128]{1,0:T(2,128)S(1)}, f32[2,128]{1,0:T(2,128)S(1)}, u32[]{:S(2)}, u32[]{:S(2)}) %collective-permute-start.1) | collective-permute-done | bytes 1056 | tf_op jit(solution)/shard_map/ppermute | solution.py:596
  13.3 0.0 collective-permute-done.refs_1_
  13.3 0.9 %first_sums.1 = (bf16[320,1152]{1,0:T(8,128)(2,1)S(1)}, f32[168,256]{1,0:T(8,128)S(1)}, f32[16,256]{1,0:T(8,128)S(1)}, f32[128]{0:T(128)}) custom-call(f32[2,128]{1,0:T(2,128)S(1)} %get-tuple-element.48.refs_0_, f32[2,128]{1,0:T(2,128)S(1)} %collective-permute-done.refs_1_, f32[2,128]{1,0:T(2,128)S(1)} %collective-permute-done.1.refs_2_, ...), custom_call_target="tpu_custom_call" | custom-call | tf_op jit(solution)/shard_map/first_sums/pallas_call | solution.py:412
  14.2 1.5 %collective-permute-start.3 = (f32[168,256]{1,0:T(8,128)S(1)}, f32[168,256]{1,0:T(8,128)S(1)}, u32[]{:S(2)}, u32[]{:S(2)}) collective-permute-start(f32[168,256]{1,0:T(8,128)S(1)} %get-tuple-element.53.send_a_ref), channel_id=1, source_target_pairs={{0,4},{4,0},{8,12},{12,8},{16,20},{20,16},{24,28},{28,24},{1,5},{5... | collective-permute-start | bytes 516104 | tf_op jit(solution)/shard_map/ppermute | solution.py:459
  15.8 0.3 second_sums.1
  16.1 0.6 %collective-permute-start.8 = (f32[168,256]{1,0:T(8,128)S(1)}, f32[168,256]{1,0:T(8,128)S(1)}, u32[]{:S(2)}, u32[]{:S(2)}) collective-permute-start(f32[168,256]{1,0:T(8,128)S(1)} %second_sums.1), channel_id=1, source_target_pairs={{0,4},{4,0},{8,12},{12,8},{16,20},{20,16},{24,28},{28,24},{1,5},{5... | collective-permute-start | bytes 516104 | tf_op jit(solution)/shard_map/ppermute | solution.py:459
  16.6 2.7 %rest_sums.1 = (f32[168,256]{1,0:T(8,128)S(1)}, f32[152,256]{1,0:T(8,128)S(1)}, f32[152,256]{1,0:T(8,128)S(1)}, f32[152,256]{1,0:T(8,128)S(1)}, f32[152,256]{1,0...) custom-call(bf16[320,1152]{1,0:T(8,128)(2,1)S(1)} %get-tuple-element, ...), custom_call_target="tpu_custom_call" | custom-call | tf_op jit(solution)/shard_map/rest_sums/pallas_call | solution.py:433
  19.3 2.2 %collective-permute-done.3.right = f32[168,256]{1,0:T(8,128)S(1)} collective-permute-done((f32[168,256]{1,0:T(8,128)S(1)}, f32[168,256]{1,0:T(8,128)S(1)}, u32[]{:S(2)}, u32[]{:S(2)}) %collective-permute-start.3) | collective-permute-done | bytes 172064 | tf_op jit(solution)/shard_map/ppermute | solution.py:459
  21.6 1.6 %collective-permute-start.5 = (f32[168,256]{1,0:T(8,128)S(1)}, f32[168,256]{1,0:T(8,128)S(1)}, u32[]{:S(2)}, u32[]{:S(2)}) collective-permute-start(f32[168,256]{1,0:T(8,128)S(1)} %join.6.sum0), channel_id=1, source_target_pairs={{0,8},{4,12},{8,0},{12,4},{16,24},{20,28},{24,16},{28,20},{1,9},{5... | collective-permute-start | bytes 516104 | tf_op jit(solution)/shard_map/ppermute | solution.py:493
  23.2 1.5 %collective-permute-start.4 = (f32[152,256]{1,0:T(8,128)S(1)}, f32[152,256]{1,0:T(8,128)S(1)}, u32[]{:S(2)}, u32[]{:S(2)}) collective-permute-start(f32[152,256]{1,0:T(8,128)S(1)} %get-tuple-element.61), channel_id=1, source_target_pairs={{0,4},{4,0},{8,12},{12,8},{16,20},{20,16},{24,28},{28,24},{1,5},{5... | collective-permute-start | bytes 466952 | tf_op jit(solution)/shard_map/ppermute | solution.py:459
  24.7 0.0 collective-permute-done.8.right
  24.8 1.6 %collective-permute-start.9 = (f32[152,256]{1,0:T(8,128)S(1)}, f32[152,256]{1,0:T(8,128)S(1)}, u32[]{:S(2)}, u32[]{:S(2)}) collective-permute-start(f32[152,256]{1,0:T(8,128)S(1)} %get-tuple-element.72), channel_id=1, source_target_pairs={{0,4},{4,0},{8,12},{12,8},{16,20},{20,16},{24,28},{28,24},{1,5},{5... | collective-permute-start | bytes 466952 | tf_op jit(solution)/shard_map/ppermute | solution.py:459
  26.4 2.0 %collective-permute-start.10 = (f32[168,256]{1,0:T(8,128)S(1)}, f32[168,256]{1,0:T(8,128)S(1)}, u32[]{:S(2)}, u32[]{:S(2)}) collective-permute-start(f32[168,256]{1,0:T(8,128)S(1)} %join.8.sum0), channel_id=1, source_target_pairs={{0,8},{4,12},{8,0},{12,4},{16,24},{20,28},{24,16},{28,20},{1,9},{5... | collective-permute-start | bytes 516104 | tf_op jit(solution)/shard_map/ppermute | solution.py:493
  28.4 0.8 %collective-permute-done.4.pair1 = f32[152,256]{1,0:T(8,128)S(1)} collective-permute-done((f32[152,256]{1,0:T(8,128)S(1)}, f32[152,256]{1,0:T(8,128)S(1)}, u32[]{:S(2)}, u32[]{:S(2)}) %collective-permute-start.4) | collective-permute-done | bytes 155680 | tf_op jit(solution)/shard_map/ppermute | solution.py:459
  29.2 0.0 collective-permute-done.5.got0
  29.2 1.6 %collective-permute-start.6 = (f32[152,256]{1,0:T(8,128)S(1)}, f32[152,256]{1,0:T(8,128)S(1)}, u32[]{:S(2)}, u32[]{:S(2)}) collective-permute-start(f32[152,256]{1,0:T(8,128)S(1)} %get-tuple-element.65), channel_id=1, source_target_pairs={{0,4},{4,0},{8,12},{12,8},{16,20},{20,16},{24,28},{28,24},{1,5},{5... | collective-permute-start | bytes 466952 | tf_op jit(solution)/shard_map/ppermute | solution.py:459
  30.8 1.4 %collective-permute-start.16 = (f32[152,256]{1,0:T(8,128)S(1)}, f32[152,256]{1,0:T(8,128)S(1)}, u32[]{:S(2)}, u32[]{:S(2)}) collective-permute-start(f32[152,256]{1,0:T(8,128)S(1)} %get-tuple-element.84.sum1), channel_id=1, source_target_pairs={{0,8},{4,12},{8,0},{12,4},{16,24},{20,28},{24,16},{28,20},{1,9},{5... | collective-permute-start | bytes 466952 | tf_op jit(solution)/shard_map/ppermute | solution.py:497
  32.3 0.0 collective-permute-start.17
  32.3 0.0 collective-permute-done.9.pair1
  32.3 0.7 %collective-permute-done.10.got0 = f32[168,256]{1,0:T(8,128)S(1)} collective-permute-done((f32[168,256]{1,0:T(8,128)S(1)}, f32[168,256]{1,0:T(8,128)S(1)}, u32[]{:S(2)}, u32[]{:S(2)}) %collective-permute-start.10) | collective-permute-done | bytes 172064 | tf_op jit(solution)/shard_map/ppermute | solution.py:493
  33.0 1.0 %collective-permute-start.11 = (f32[152,256]{1,0:T(8,128)S(1)}, f32[152,256]{1,0:T(8,128)S(1)}, u32[]{:S(2)}, u32[]{:S(2)}) collective-permute-start(f32[152,256]{1,0:T(8,128)S(1)} %get-tuple-element.76), channel_id=1, source_target_pairs={{0,4},{4,0},{8,12},{12,8},{16,20},{20,16},{24,28},{28,24},{1,5},{5... | collective-permute-start | bytes 466952 | tf_op jit(solution)/shard_map/ppermute | solution.py:459
  34.0 2.0 %collective-permute-start.12 = (f32[152,256]{1,0:T(8,128)S(1)}, f32[152,256]{1,0:T(8,128)S(1)}, u32[]{:S(2)}, u32[]{:S(2)}) collective-permute-start(f32[152,256]{1,0:T(8,128)S(1)} %get-tuple-element.77.sum1), channel_id=1, source_target_pairs={{0,8},{4,12},{8,0},{12,4},{16,24},{20,28},{24,16},{28,20},{1,9},{5... | collective-permute-start | bytes 466952 | tf_op jit(solution)/shard_map/ppermute | solution.py:497
  36.0 0.0 collective-permute-done.6.pair2
  36.1 0.0 collective-permute-start.13
  36.1 0.5 collective-permute-done.16.got1
  36.5 1.1 %collective-permute-start.7 = (f32[304,256]{1,0:T(8,128)S(1)}, f32[304,256]{1,0:T(8,128)S(1)}, u32[]{:S(2)}, u32[]{:S(2)}) collective-permute-start(f32[304,256]{1,0:T(8,128)S(1)} %get-tuple-element.66), channel_id=1, source_target_pairs={{0,4},{4,0},{8,12},{12,8},{16,20},{20,16},{24,28},{28,24},{1,5},{5... | collective-permute-start | bytes 933896 | tf_op jit(solution)/shard_map/ppermute | solution.py:459
  37.6 0.0 collective-permute-done.17.got2
  37.7 2.6 %collective-permute-start.18 = (f32[168,256]{1,0:T(8,128)S(1)}, f32[168,256]{1,0:T(8,128)S(1)}, u32[]{:S(2)}, u32[]{:S(2)}) collective-permute-start(f32[168,256]{1,0:T(8,128)S(1)} %get-tuple-element.86.refs_2_), channel_id=1, source_target_pairs={{0,8},{4,12},{8,0},{12,4},{16,24},{20,28},{24,16},{28,20},{1,9},{5... | collective-permute-start | bytes 516104 | tf_op jit(solution)/shard_map/ppermute | solution.py:502
  40.3 0.0 collective-permute-done.11.pair2
  40.3 0.0 collective-permute-done.12.got1
  40.4 0.0 collective-permute-done.13.got2
  40.4 2.2 %collective-permute-start.14 = (f32[168,256]{1,0:T(8,128)S(1)}, f32[168,256]{1,0:T(8,128)S(1)}, u32[]{:S(2)}, u32[]{:S(2)}) collective-permute-start(f32[168,256]{1,0:T(8,128)S(1)} %get-tuple-element.79.refs_2_), channel_id=1, source_target_pairs={{0,8},{4,12},{8,0},{12,4},{16,24},{20,28},{24,16},{28,20},{1,9},{5... | collective-permute-start | bytes 516104 | tf_op jit(solution)/shard_map/ppermute | solution.py:502
  42.6 0.0 collective-permute-start.19
  42.6 0.5 %collective-permute-start.15 = (f32[152,256]{1,0:T(8,128)S(1)}, f32[152,256]{1,0:T(8,128)S(1)}, u32[]{:S(2)}, u32[]{:S(2)}) collective-permute-start(f32[152,256]{1,0:T(8,128)S(1)} %get-tuple-element.80), channel_id=1, source_target_pairs={{0,1},{1,0},{2,3},{3,2},{4,5},{5,4},{6,7},{7,6},{8,16},{9,17},{10,... | collective-permute-start | bytes 466952 | tf_op jit(solution)/shard_map/ppermute | solution.py:503
  43.1 0.9 %collective-permute-done.19.refs_4_ = f32[152,256]{1,0:T(8,128)S(1)} collective-permute-done((f32[152,256]{1,0:T(8,128)S(1)}, f32[152,256]{1,0:T(8,128)S(1)}, u32[]{:S(2)}, u32[]{:S(2)}) %collective-permute-start.19) | collective-permute-done | bytes 155680 | tf_op jit(solution)/shard_map/ppermute | solution.py:503
  44.0 1.6 %collective-permute-done.18.refs_3_ = f32[168,256]{1,0:T(8,128)S(1)} collective-permute-done((f32[168,256]{1,0:T(8,128)S(1)}, f32[168,256]{1,0:T(8,128)S(1)}, u32[]{:S(2)}, u32[]{:S(2)}) %collective-permute-start.18) | collective-permute-done | bytes 172064 | tf_op jit(solution)/shard_map/ppermute | solution.py:502
  45.6 0.2 collective-permute-done.7.refs_1_
  45.8 1.2 %last_ratio.2 = (f32[25,3072]{1,0:T(8,128)S(1)}, f32[1,25]{1,0:T(1,128)S(1)}) custom-call(f32[152,256]{1,0:T(8,128)S(1)} %get-tuple-element.82.refs_0_, f32[304,256]{1,0:T(8,128)S(1)} %collective-permute-done.7.refs_1_, f32[168,256]{1,0:T(8,128)S(1)} %get-tuple-element.86.refs_2_, f32[168,256]{1,0:T(8,128)S(1)} %collective-permute-done.18.refs_3_, ...), custom_call_target="tpu_custom_call" | custom-call | flops 1000 | tf_op jit(solution)/shard_map/last_ratio/pallas_call | solution.py:518
  47.0 0.0 collective-permute-done.15.refs_4_
  47.0 0.9 %collective-permute-done.14.refs_3_ = f32[168,256]{1,0:T(8,128)S(1)} collective-permute-done((f32[168,256]{1,0:T(8,128)S(1)}, f32[168,256]{1,0:T(8,128)S(1)}, u32[]{:S(2)}, u32[]{:S(2)}) %collective-permute-start.14) | collective-permute-done | bytes 172064 | tf_op jit(solution)/shard_map/ppermute | solution.py:502
  47.9 1.9 %last_ratio.3 = (f32[25,3072]{1,0:T(8,128)}, f32[25]{0:T(128)}) custom-call(f32[152,256]{1,0:T(8,128)S(1)} %get-tuple-element.55.refs_0_, f32[304,256]{1,0:T(8,128)S(1)} %collective-permute-done.7.refs_1_, f32[168,256]{1,0:T(8,128)S(1)} %get-tuple-element.79.refs_2_, f32[168,256]{1,0:T(8,128)S(1)} %collective-permute-done.14.refs_3_, ...), custom_call_target="tpu_custom_call" | custom-call | flops 1000 | tf_op jit(solution)/shard_map/last_ratio/pallas_call | solution.py:518
  (6 shorter events, 0.2 us)
Async XLA Ops:
  7.3 3.7 %collective-permute-start.2 = (f32[2,128]{1,0:T(2,128)S(1)}, f32[2,128]{1,0:T(2,128)S(1)}, u32[]{:S(2)}, u32[]{:S(2)}) collective-permute-start(f32[2,128]{1,0:T(2,128)S(1)} %get-tuple-element.48.refs_0_), channel_id=1, source_target_pairs={{0,3},{1,2},{2,1},{3,0},{4,7},{5,6},{6,5},{7,4},{8,11},{9,10},{10,... | collective-permute-start | bytes 3080 | tf_op jit(solution)/shard_map/ppermute | solution.py:596
  9.8 3.6 %collective-permute-start.1 = (f32[2,128]{1,0:T(2,128)S(1)}, f32[2,128]{1,0:T(2,128)S(1)}, u32[]{:S(2)}, u32[]{:S(2)}) collective-permute-start(f32[2,128]{1,0:T(2,128)S(1)} %get-tuple-element.48.refs_0_), channel_id=1, source_target_pairs={{0,2},{1,3},{2,0},{3,1},{4,6},{5,7},{6,4},{7,5},{8,10},{9,11},{10,... | collective-permute-start | bytes 3080 | tf_op jit(solution)/shard_map/ppermute | solution.py:596
  10.4 2.9 %collective-permute-start = (f32[2,128]{1,0:T(2,128)S(1)}, f32[2,128]{1,0:T(2,128)S(1)}, u32[]{:S(2)}, u32[]{:S(2)}) collective-permute-start(f32[2,128]{1,0:T(2,128)S(1)} %get-tuple-element.48.refs_0_), channel_id=1, source_target_pairs={{0,1},{1,0},{2,3},{3,2},{4,5},{5,4},{6,7},{7,6},{8,9},{9,8},{10,11... | collective-permute-start | bytes 3080 | tf_op jit(solution)/shard_map/ppermute | solution.py:596
  14.2 7.3 %collective-permute-start.3 = (f32[168,256]{1,0:T(8,128)S(1)}, f32[168,256]{1,0:T(8,128)S(1)}, u32[]{:S(2)}, u32[]{:S(2)}) collective-permute-start(f32[168,256]{1,0:T(8,128)S(1)} %get-tuple-element.53.send_a_ref), channel_id=1, source_target_pairs={{0,4},{4,0},{8,12},{12,8},{16,20},{20,16},{24,28},{28,24},{1,5},{5... | collective-permute-start | bytes 516104 | tf_op jit(solution)/shard_map/ppermute | solution.py:459
  16.1 8.7 %collective-permute-start.8 = (f32[168,256]{1,0:T(8,128)S(1)}, f32[168,256]{1,0:T(8,128)S(1)}, u32[]{:S(2)}, u32[]{:S(2)}) collective-permute-start(f32[168,256]{1,0:T(8,128)S(1)} %second_sums.1), channel_id=1, source_target_pairs={{0,4},{4,0},{8,12},{12,8},{16,20},{20,16},{24,28},{28,24},{1,5},{5... | collective-permute-start | bytes 516104 | tf_op jit(solution)/shard_map/ppermute | solution.py:459
  21.6 7.6 %collective-permute-start.5 = (f32[168,256]{1,0:T(8,128)S(1)}, f32[168,256]{1,0:T(8,128)S(1)}, u32[]{:S(2)}, u32[]{:S(2)}) collective-permute-start(f32[168,256]{1,0:T(8,128)S(1)} %join.6.sum0), channel_id=1, source_target_pairs={{0,8},{4,12},{8,0},{12,4},{16,24},{20,28},{24,16},{28,20},{1,9},{5... | collective-permute-start | bytes 516104 | tf_op jit(solution)/shard_map/ppermute | solution.py:493
  23.2 6.0 %collective-permute-start.4 = (f32[152,256]{1,0:T(8,128)S(1)}, f32[152,256]{1,0:T(8,128)S(1)}, u32[]{:S(2)}, u32[]{:S(2)}) collective-permute-start(f32[152,256]{1,0:T(8,128)S(1)} %get-tuple-element.61), channel_id=1, source_target_pairs={{0,4},{4,0},{8,12},{12,8},{16,20},{20,16},{24,28},{28,24},{1,5},{5... | collective-permute-start | bytes 466952 | tf_op jit(solution)/shard_map/ppermute | solution.py:459
  24.8 7.5 %collective-permute-start.9 = (f32[152,256]{1,0:T(8,128)S(1)}, f32[152,256]{1,0:T(8,128)S(1)}, u32[]{:S(2)}, u32[]{:S(2)}) collective-permute-start(f32[152,256]{1,0:T(8,128)S(1)} %get-tuple-element.72), channel_id=1, source_target_pairs={{0,4},{4,0},{8,12},{12,8},{16,20},{20,16},{24,28},{28,24},{1,5},{5... | collective-permute-start | bytes 466952 | tf_op jit(solution)/shard_map/ppermute | solution.py:459
  26.4 6.6 %collective-permute-start.10 = (f32[168,256]{1,0:T(8,128)S(1)}, f32[168,256]{1,0:T(8,128)S(1)}, u32[]{:S(2)}, u32[]{:S(2)}) collective-permute-start(f32[168,256]{1,0:T(8,128)S(1)} %join.8.sum0), channel_id=1, source_target_pairs={{0,8},{4,12},{8,0},{12,4},{16,24},{20,28},{24,16},{28,20},{1,9},{5... | collective-permute-start | bytes 516104 | tf_op jit(solution)/shard_map/ppermute | solution.py:493
  29.2 6.8 %collective-permute-start.6 = (f32[152,256]{1,0:T(8,128)S(1)}, f32[152,256]{1,0:T(8,128)S(1)}, u32[]{:S(2)}, u32[]{:S(2)}) collective-permute-start(f32[152,256]{1,0:T(8,128)S(1)} %get-tuple-element.65), channel_id=1, source_target_pairs={{0,4},{4,0},{8,12},{12,8},{16,20},{20,16},{24,28},{28,24},{1,5},{5... | collective-permute-start | bytes 466952 | tf_op jit(solution)/shard_map/ppermute | solution.py:459
  30.8 5.7 %collective-permute-start.16 = (f32[152,256]{1,0:T(8,128)S(1)}, f32[152,256]{1,0:T(8,128)S(1)}, u32[]{:S(2)}, u32[]{:S(2)}) collective-permute-start(f32[152,256]{1,0:T(8,128)S(1)} %get-tuple-element.84.sum1), channel_id=1, source_target_pairs={{0,8},{4,12},{8,0},{12,4},{16,24},{20,28},{24,16},{28,20},{1,9},{5... | collective-permute-start | bytes 466952 | tf_op jit(solution)/shard_map/ppermute | solution.py:497
  32.3 5.4 %collective-permute-start.17 = (f32[168,256]{1,0:T(8,128)S(1)}, f32[168,256]{1,0:T(8,128)S(1)}, u32[]{:S(2)}, u32[]{:S(2)}) collective-permute-start(f32[168,256]{1,0:T(8,128)S(1)} %get-tuple-element.85.both0), channel_id=1, source_target_pairs={{0,1},{1,0},{2,3},{3,2},{4,5},{5,4},{6,7},{7,6},{8,16},{9,17},{10,... | collective-permute-start | bytes 516104 | tf_op jit(solution)/shard_map/ppermute | solution.py:498
  33.0 7.3 %collective-permute-start.11 = (f32[152,256]{1,0:T(8,128)S(1)}, f32[152,256]{1,0:T(8,128)S(1)}, u32[]{:S(2)}, u32[]{:S(2)}) collective-permute-start(f32[152,256]{1,0:T(8,128)S(1)} %get-tuple-element.76), channel_id=1, source_target_pairs={{0,4},{4,0},{8,12},{12,8},{16,20},{20,16},{24,28},{28,24},{1,5},{5... | collective-permute-start | bytes 466952 | tf_op jit(solution)/shard_map/ppermute | solution.py:459
  34.0 6.3 %collective-permute-start.12 = (f32[152,256]{1,0:T(8,128)S(1)}, f32[152,256]{1,0:T(8,128)S(1)}, u32[]{:S(2)}, u32[]{:S(2)}) collective-permute-start(f32[152,256]{1,0:T(8,128)S(1)} %get-tuple-element.77.sum1), channel_id=1, source_target_pairs={{0,8},{4,12},{8,0},{12,4},{16,24},{20,28},{24,16},{28,20},{1,9},{5... | collective-permute-start | bytes 466952 | tf_op jit(solution)/shard_map/ppermute | solution.py:497
  36.1 4.3 %collective-permute-start.13 = (f32[168,256]{1,0:T(8,128)S(1)}, f32[168,256]{1,0:T(8,128)S(1)}, u32[]{:S(2)}, u32[]{:S(2)}) collective-permute-start(f32[168,256]{1,0:T(8,128)S(1)} %get-tuple-element.78.both0), channel_id=1, source_target_pairs={{0,1},{1,0},{2,3},{3,2},{4,5},{5,4},{6,7},{7,6},{8,16},{9,17},{10,... | collective-permute-start | bytes 516104 | tf_op jit(solution)/shard_map/ppermute | solution.py:498
  36.5 9.3 %collective-permute-start.7 = (f32[304,256]{1,0:T(8,128)S(1)}, f32[304,256]{1,0:T(8,128)S(1)}, u32[]{:S(2)}, u32[]{:S(2)}) collective-permute-start(f32[304,256]{1,0:T(8,128)S(1)} %get-tuple-element.66), channel_id=1, source_target_pairs={{0,4},{4,0},{8,12},{12,8},{16,20},{20,16},{24,28},{28,24},{1,5},{5... | collective-permute-start | bytes 933896 | tf_op jit(solution)/shard_map/ppermute | solution.py:459
  37.7 7.9 %collective-permute-start.18 = (f32[168,256]{1,0:T(8,128)S(1)}, f32[168,256]{1,0:T(8,128)S(1)}, u32[]{:S(2)}, u32[]{:S(2)}) collective-permute-start(f32[168,256]{1,0:T(8,128)S(1)} %get-tuple-element.86.refs_2_), channel_id=1, source_target_pairs={{0,8},{4,12},{8,0},{12,4},{16,24},{20,28},{24,16},{28,20},{1,9},{5... | collective-permute-start | bytes 516104 | tf_op jit(solution)/shard_map/ppermute | solution.py:502
  40.4 7.5 %collective-permute-start.14 = (f32[168,256]{1,0:T(8,128)S(1)}, f32[168,256]{1,0:T(8,128)S(1)}, u32[]{:S(2)}, u32[]{:S(2)}) collective-permute-start(f32[168,256]{1,0:T(8,128)S(1)} %get-tuple-element.79.refs_2_), channel_id=1, source_target_pairs={{0,8},{4,12},{8,0},{12,4},{16,24},{20,28},{24,16},{28,20},{1,9},{5... | collective-permute-start | bytes 516104 | tf_op jit(solution)/shard_map/ppermute | solution.py:502
  42.6 1.4 %collective-permute-start.19 = (f32[152,256]{1,0:T(8,128)S(1)}, f32[152,256]{1,0:T(8,128)S(1)}, u32[]{:S(2)}, u32[]{:S(2)}) collective-permute-start(f32[152,256]{1,0:T(8,128)S(1)} %get-tuple-element.87), channel_id=1, source_target_pairs={{0,1},{1,0},{2,3},{3,2},{4,5},{5,4},{6,7},{7,6},{8,16},{9,17},{10,... | collective-permute-start | bytes 466952 | tf_op jit(solution)/shard_map/ppermute | solution.py:503
  42.6 4.4 %collective-permute-start.15 = (f32[152,256]{1,0:T(8,128)S(1)}, f32[152,256]{1,0:T(8,128)S(1)}, u32[]{:S(2)}, u32[]{:S(2)}) collective-permute-start(f32[152,256]{1,0:T(8,128)S(1)} %get-tuple-element.80), channel_id=1, source_target_pairs={{0,1},{1,0},{2,3},{3,2},{4,5},{5,4},{6,7},{7,6},{8,16},{9,17},{10,... | collective-permute-start | bytes 466952 | tf_op jit(solution)/shard_map/ppermute | solution.py:503

commit v3 on v2

--- a/solution.py
+++ b/solution.py
@@ -20,12 +20,15 @@
     return -(-value // multiple) * multiple
 
 
-def thirds(value, axis):
+def split(value):
     high = value.astype(BF16)
     rest = value - high.astype(F32)
     middle = rest.astype(BF16)
-    low = (rest - middle.astype(F32)).astype(BF16)
-    return jnp.concatenate([high, middle, low], axis=axis)
+    return high, middle, (rest - middle.astype(F32)).astype(BF16)
+
+
+def thirds(value, axis):
+    return jnp.concatenate(split(value), axis=axis)
 
 
 def estep_kernel(
@@ -91,18 +94,16 @@
     def build(shifts):
         for at in range(0, count, 16):
             for lane in range(0, fpix, 128):
-                real = images_ref[at : at + 16, lane : lane + 128].astype(F32)
-                imag = images_ref[at : at + 16, fpix + lane : fpix + lane + 128].astype(F32)
                 cw = cw_ref[at : at + 16, lane : lane + 128]
+                real = images_ref[at : at + 16, lane : lane + 128].astype(F32) * cw
+                imag = images_ref[at : at + 16, fpix + lane : fpix + lane + 128].astype(F32) * cw
                 for s in shifts:
                     c = cos_ref[s : s + 1, lane : lane + 128]
                     d = sin_ref[s : s + 1, lane : lane + 128]
                     to = s * count + at
-                    copies_ref[to : to + 16, lane : lane + 128] = (
-                        (real * c + imag * d) * cw
-                    ).astype(BF16)
+                    copies_ref[to : to + 16, lane : lane + 128] = (real * c + imag * d).astype(BF16)
                     copies_ref[to : to + 16, fpix + lane : fpix + lane + 128] = (
-                        (imag * c - real * d) * cw
+                        imag * c - real * d
                     ).astype(BF16)
 
     for load in loads[5:]:
@@ -118,10 +119,12 @@
     low = (power - high.astype(F32)).astype(BF16)
     c2w = thirds(c2w, 0)
     norms = lax.dot_general(
-        high, c2w, (((1,), (1,)), ((), ())), preferred_element_type=F32
-    ) + lax.dot_general(low, c2w, (((1,), (1,)), ((), ())), preferred_element_type=F32)
-    norms = norms[:, :ngroup] + norms[:, ngroup : 2 * ngroup] + norms[:, 2 * ngroup :]
-    norm_img = jnp.dot(thirds(norms, 1), three, preferred_element_type=F32)
+        c2w, high, (((1,), (1,)), ((), ())), preferred_element_type=F32
+    ) + lax.dot_general(c2w, low, (((1,), (1,)), ((), ())), preferred_element_type=F32)
+    norms = norms[:ngroup] + norms[ngroup : 2 * ngroup] + norms[2 * ngroup :]
+    norm_img = lax.dot_general(
+        thirds(norms, 0), three, (((0,), (0,)), ((), ())), preferred_element_type=F32
+    )
     row = lax.broadcasted_iota(jnp.int32, (rpad, 1), 0)
     row = jnp.where(row < hpad, row, row - hpad + half)
     valid = (row < half) | ((row >= half) & (lax.broadcasted_iota(jnp.int32, (rpad, 1), 0) >= hpad))
@@ -336,8 +339,13 @@
     z = lax.axis_index("dom") // PAIR
     end = (z == 0) | (z == LINE - 1)
     mass = jnp.where(end, line_ref[send:, :], own_ref[send:, :])
+    mass_high, mass_middle, mass_low = split(mass)
+    high, middle, low = split(share_ref[...])
     den = lax.dot_general(
-        mass, share_ref[...], (((0,), (0,)), ((), ())), precision=HI, preferred_element_type=F32
+        jnp.concatenate([mass_high] * 3 + [mass_middle] * 2 + [mass_low], axis=0),
+        jnp.concatenate([high, middle, low, high, middle, high], axis=0),
+        (((0,), (0,)), ((), ())),
+        preferred_element_type=F32,
     )
     num = keep_ref[...] + pair_ref[chain * send : (chain + 1) * send, :] + line_ref[0:send, :]
     num = num + jnp.where(end, 0.0, cross_ref[...])
@@ -387,8 +395,10 @@
     place = place - classes * jnp.floor((place + 0.5) * (1.0 / classes))
     member = ((place == mcol.astype(F32)) & (mrow < mine * classes)).astype(F32)
     share = jnp.dot(
-        jnp.sum(mass, axis=0, keepdims=True), member, precision=HI, preferred_element_type=F32
-    )
+        thirds(jnp.sum(mass, axis=0, keepdims=True), 0), member.astype(BF16),
+        preferred_element_type=F32,
+    )
+    share = jnp.sum(share, axis=0, keepdims=True)
     if before:
         share = share + before[1][...]
         frac_ref[...] = (share / images).reshape(classes)

time: 50 us -> 48.9 us (0.978)
  Pallas kernels: 13.9 us -> 12.4 us
  waiting for transfers between devices: 10.6 us -> 11.1 us
    pallas_call x2, Pallas kernels: 3.13 us -> 2.17 us  [line_path(): pl.pallas_call(last, out_shape=(jax.ShapeDtypeStruct((classes, width * ro...]
    pallas_call x1, Pallas kernels: 6.69 us -> 6.08 us  [estep(): pl.pallas_call(estep_kernel, out_shape=(jax.ShapeDtypeStruct((rpad, nshif...]
  transfers between devices with their start and end apart: 20 -> 20, of which waited for: 10 -> 10; matrix products, arithmetic and copies ran while one was open for 0% -> 0% of each run, Pallas kernels for 9% -> 8%
where the time goes in v3:
time: 48.9 us; the launch traced here: 48.7 us
  starting transfers between devices  24.6 us (50%)
  Pallas kernels  12.4 us (25%)
  waiting for transfers between devices  11.1 us (23%)
  between operations  0.71 us (1%)
    ppermute x7, starting transfers between devices, swap(): return lax.ppermute(value, 'dom', across)  8.9 us
    pallas_call x1, Pallas kernels, estep(): pl.pallas_call(estep_kernel, out_shape=(jax.ShapeDtypeStruct((rpad, nshif...  6.08 us
    ppermute x2, starting transfers between devices, reduce_chain(): line = lax.ppermute(to_ends, 'dom', outer)  4.87 us
    ppermute x2, starting transfers between devices, reduce_chain(): got0 = lax.ppermute(sum0, 'dom', outer)  3.69 us
    ppermute x2, starting transfers between devices, reduce_chain(): got1 = lax.ppermute(sum1, 'dom', outer)  3.46 us
    ppermute x7, waiting for transfers between devices, swap(): return lax.ppermute(value, 'dom', across)  3.23 us
    ppermute x3, starting transfers between devices, local(): lax.ppermute(stat, 'cls', [(c, c ^ other) for c in range(cls_n)])  3.12 us
    ppermute x2, waiting for transfers between devices, reduce_chain(): line = lax.ppermute(to_ends, 'dom', outer)  2.93 us
  transfers between devices with their start and end apart: 20, of which 10 were waited for; matrix products, arithmetic and copies ran while one was open for 0% of the time, Pallas kernels for 8%

profile of v3, /device:TPU:0, one launch (start us, length us, event | category | flops | bytes accessed | tf_op | source)
XLA Modules:
  0.0 48.7 jit_solution(1388487897009085138)
XLA Ops:
  0.6 6.1 %estep.1 = (f32[320,1152]{1,0:T(8,128)S(1)}, bf16[1152,2048]{1,0:T(8,128)(2,1)S(1)}, f32[2,128]{1,0:T(2,128)S(1)}, f32[16,128]{1,0:T(8,128)S(1)}, f32[16,256]{1,0:T(8,128)S(1)}) custom-call(bf16[128,2048]{1,0:T(8,128)(2,1)} %images_hbm.1, bf16[12,25,2048]{2,1,0:T(8,128)(2,1)} %bitcast.2, f32[16,1024]{1,0:T(8,128)} %ctf_hbm.1, f32[16,1024]{1,0:T(8,128)} %inv_hbm.1, ...), custom_call_target="tpu_custom_call" | custom-call | tf_op jit(solution)/shard_map/estep/pallas_call | solution.py:181
  6.7 2.4 %collective-permute-start.2 = (f32[2,128]{1,0:T(2,128)S(1)}, f32[2,128]{1,0:T(2,128)S(1)}, u32[]{:S(2)}, u32[]{:S(2)}) collective-permute-start(f32[2,128]{1,0:T(2,128)S(1)} %get-tuple-element.48.refs_0_), channel_id=1, source_target_pairs={{0,3},{1,2},{2,1},{3,0},{4,7},{5,6},{6,5},{7,4},{8,11},{9,10},{10,... | collective-permute-start | bytes 3080 | tf_op jit(solution)/shard_map/ppermute | solution.py:606
  9.2 0.6 %collective-permute-start.1 = (f32[2,128]{1,0:T(2,128)S(1)}, f32[2,128]{1,0:T(2,128)S(1)}, u32[]{:S(2)}, u32[]{:S(2)}) collective-permute-start(f32[2,128]{1,0:T(2,128)S(1)} %get-tuple-element.48.refs_0_), channel_id=1, source_target_pairs={{0,2},{1,3},{2,0},{3,1},{4,6},{5,7},{6,4},{7,5},{8,10},{9,11},{10,... | collective-permute-start | bytes 3080 | tf_op jit(solution)/shard_map/ppermute | solution.py:606
  9.8 0.0 collective-permute-start
  9.8 0.6 %collective-permute-done.2.refs_3_ = f32[2,128]{1,0:T(2,128)S(1)} collective-permute-done((f32[2,128]{1,0:T(2,128)S(1)}, f32[2,128]{1,0:T(2,128)S(1)}, u32[]{:S(2)}, u32[]{:S(2)}) %collective-permute-start.2) | collective-permute-done | bytes 1056 | tf_op jit(solution)/shard_map/ppermute | solution.py:606
  10.5 2.3 %collective-permute-done.1.refs_2_ = f32[2,128]{1,0:T(2,128)S(1)} collective-permute-done((f32[2,128]{1,0:T(2,128)S(1)}, f32[2,128]{1,0:T(2,128)S(1)}, u32[]{:S(2)}, u32[]{:S(2)}) %collective-permute-start.1) | collective-permute-done | bytes 1056 | tf_op jit(solution)/shard_map/ppermute | solution.py:606
  12.7 0.0 collective-permute-done.refs_1_
  12.7 0.9 %first_sums.1 = (bf16[320,1152]{1,0:T(8,128)(2,1)S(1)}, f32[168,256]{1,0:T(8,128)S(1)}, f32[16,256]{1,0:T(8,128)S(1)}, f32[128]{0:T(128)}) custom-call(f32[2,128]{1,0:T(2,128)S(1)} %get-tuple-element.48.refs_0_, f32[2,128]{1,0:T(2,128)S(1)} %collective-permute-done.refs_1_, f32[2,128]{1,0:T(2,128)S(1)} %collective-permute-done.1.refs_2_, ...), custom_call_target="tpu_custom_call" | custom-call | tf_op jit(solution)/shard_map/first_sums/pallas_call | solution.py:422
  13.6 1.5 %collective-permute-start.3 = (f32[168,256]{1,0:T(8,128)S(1)}, f32[168,256]{1,0:T(8,128)S(1)}, u32[]{:S(2)}, u32[]{:S(2)}) collective-permute-start(f32[168,256]{1,0:T(8,128)S(1)} %get-tuple-element.53.send_a_ref), channel_id=1, source_target_pairs={{0,4},{4,0},{8,12},{12,8},{16,20},{20,16},{24,28},{28,24},{1,5},{5... | collective-permute-start | bytes 516104 | tf_op jit(solution)/shard_map/ppermute | solution.py:469
  15.1 0.3 second_sums.1
  15.4 0.6 %collective-permute-start.8 = (f32[168,256]{1,0:T(8,128)S(1)}, f32[168,256]{1,0:T(8,128)S(1)}, u32[]{:S(2)}, u32[]{:S(2)}) collective-permute-start(f32[168,256]{1,0:T(8,128)S(1)} %second_sums.1), channel_id=1, source_target_pairs={{0,4},{4,0},{8,12},{12,8},{16,20},{20,16},{24,28},{28,24},{1,5},{5... | collective-permute-start | bytes 516104 | tf_op jit(solution)/shard_map/ppermute | solution.py:469
  16.0 2.7 %rest_sums.1 = (f32[168,256]{1,0:T(8,128)S(1)}, f32[152,256]{1,0:T(8,128)S(1)}, f32[152,256]{1,0:T(8,128)S(1)}, f32[152,256]{1,0:T(8,128)S(1)}, f32[152,256]{1,0...) custom-call(bf16[320,1152]{1,0:T(8,128)(2,1)S(1)} %get-tuple-element, ...), custom_call_target="tpu_custom_call" | custom-call | tf_op jit(solution)/shard_map/rest_sums/pallas_call | solution.py:443
  18.7 2.2 %collective-permute-done.3.right = f32[168,256]{1,0:T(8,128)S(1)} collective-permute-done((f32[168,256]{1,0:T(8,128)S(1)}, f32[168,256]{1,0:T(8,128)S(1)}, u32[]{:S(2)}, u32[]{:S(2)}) %collective-permute-start.3) | collective-permute-done | bytes 172064 | tf_op jit(solution)/shard_map/ppermute | solution.py:469
  21.0 1.6 %collective-permute-start.5 = (f32[168,256]{1,0:T(8,128)S(1)}, f32[168,256]{1,0:T(8,128)S(1)}, u32[]{:S(2)}, u32[]{:S(2)}) collective-permute-start(f32[168,256]{1,0:T(8,128)S(1)} %join.6.sum0), channel_id=1, source_target_pairs={{0,8},{4,12},{8,0},{12,4},{16,24},{20,28},{24,16},{28,20},{1,9},{5... | collective-permute-start | bytes 516104 | tf_op jit(solution)/shard_map/ppermute | solution.py:503
  22.6 1.5 %collective-permute-start.4 = (f32[152,256]{1,0:T(8,128)S(1)}, f32[152,256]{1,0:T(8,128)S(1)}, u32[]{:S(2)}, u32[]{:S(2)}) collective-permute-start(f32[152,256]{1,0:T(8,128)S(1)} %get-tuple-element.61), channel_id=1, source_target_pairs={{0,4},{4,0},{8,12},{12,8},{16,20},{20,16},{24,28},{28,24},{1,5},{5... | collective-permute-start | bytes 466952 | tf_op jit(solution)/shard_map/ppermute | solution.py:469
  24.1 0.0 collective-permute-done.8.right
  24.2 1.6 %collective-permute-start.9 = (f32[152,256]{1,0:T(8,128)S(1)}, f32[152,256]{1,0:T(8,128)S(1)}, u32[]{:S(2)}, u32[]{:S(2)}) collective-permute-start(f32[152,256]{1,0:T(8,128)S(1)} %get-tuple-element.72), channel_id=1, source_target_pairs={{0,4},{4,0},{8,12},{12,8},{16,20},{20,16},{24,28},{28,24},{1,5},{5... | collective-permute-start | bytes 466952 | tf_op jit(solution)/shard_map/ppermute | solution.py:469
  25.8 2.0 %collective-permute-start.10 = (f32[168,256]{1,0:T(8,128)S(1)}, f32[168,256]{1,0:T(8,128)S(1)}, u32[]{:S(2)}, u32[]{:S(2)}) collective-permute-start(f32[168,256]{1,0:T(8,128)S(1)} %join.8.sum0), channel_id=1, source_target_pairs={{0,8},{4,12},{8,0},{12,4},{16,24},{20,28},{24,16},{28,20},{1,9},{5... | collective-permute-start | bytes 516104 | tf_op jit(solution)/shard_map/ppermute | solution.py:503
  27.8 0.8 %collective-permute-done.4.pair1 = f32[152,256]{1,0:T(8,128)S(1)} collective-permute-done((f32[152,256]{1,0:T(8,128)S(1)}, f32[152,256]{1,0:T(8,128)S(1)}, u32[]{:S(2)}, u32[]{:S(2)}) %collective-permute-start.4) | collective-permute-done | bytes 155680 | tf_op jit(solution)/shard_map/ppermute | solution.py:469
  28.6 0.0 collective-permute-done.5.got0
  28.6 1.6 %collective-permute-start.6 = (f32[152,256]{1,0:T(8,128)S(1)}, f32[152,256]{1,0:T(8,128)S(1)}, u32[]{:S(2)}, u32[]{:S(2)}) collective-permute-start(f32[152,256]{1,0:T(8,128)S(1)} %get-tuple-element.65), channel_id=1, source_target_pairs={{0,4},{4,0},{8,12},{12,8},{16,20},{20,16},{24,28},{28,24},{1,5},{5... | collective-permute-start | bytes 466952 | tf_op jit(solution)/shard_map/ppermute | solution.py:469
  30.2 1.4 %collective-permute-start.16 = (f32[152,256]{1,0:T(8,128)S(1)}, f32[152,256]{1,0:T(8,128)S(1)}, u32[]{:S(2)}, u32[]{:S(2)}) collective-permute-start(f32[152,256]{1,0:T(8,128)S(1)} %get-tuple-element.84.sum1), channel_id=1, source_target_pairs={{0,8},{4,12},{8,0},{12,4},{16,24},{20,28},{24,16},{28,20},{1,9},{5... | collective-permute-start | bytes 466952 | tf_op jit(solution)/shard_map/ppermute | solution.py:507
  31.7 0.0 collective-permute-start.17
  31.7 0.0 collective-permute-done.9.pair1
  31.7 0.7 %collective-permute-done.10.got0 = f32[168,256]{1,0:T(8,128)S(1)} collective-permute-done((f32[168,256]{1,0:T(8,128)S(1)}, f32[168,256]{1,0:T(8,128)S(1)}, u32[]{:S(2)}, u32[]{:S(2)}) %collective-permute-start.10) | collective-permute-done | bytes 172064 | tf_op jit(solution)/shard_map/ppermute | solution.py:503
  32.4 1.0 %collective-permute-start.11 = (f32[152,256]{1,0:T(8,128)S(1)}, f32[152,256]{1,0:T(8,128)S(1)}, u32[]{:S(2)}, u32[]{:S(2)}) collective-permute-start(f32[152,256]{1,0:T(8,128)S(1)} %get-tuple-element.76), channel_id=1, source_target_pairs={{0,4},{4,0},{8,12},{12,8},{16,20},{20,16},{24,28},{28,24},{1,5},{5... | collective-permute-start | bytes 466952 | tf_op jit(solution)/shard_map/ppermute | solution.py:469
  33.4 2.0 %collective-permute-start.12 = (f32[152,256]{1,0:T(8,128)S(1)}, f32[152,256]{1,0:T(8,128)S(1)}, u32[]{:S(2)}, u32[]{:S(2)}) collective-permute-start(f32[152,256]{1,0:T(8,128)S(1)} %get-tuple-element.77.sum1), channel_id=1, source_target_pairs={{0,8},{4,12},{8,0},{12,4},{16,24},{20,28},{24,16},{28,20},{1,9},{5... | collective-permute-start | bytes 466952 | tf_op jit(solution)/shard_map/ppermute | solution.py:507
  35.4 0.0 collective-permute-done.6.pair2
  35.4 0.0 collective-permute-start.13
  35.4 0.4 collective-permute-done.16.got1
  35.9 1.1 %collective-permute-start.7 = (f32[304,256]{1,0:T(8,128)S(1)}, f32[304,256]{1,0:T(8,128)S(1)}, u32[]{:S(2)}, u32[]{:S(2)}) collective-permute-start(f32[304,256]{1,0:T(8,128)S(1)} %get-tuple-element.66), channel_id=1, source_target_pairs={{0,4},{4,0},{8,12},{12,8},{16,20},{20,16},{24,28},{28,24},{1,5},{5... | collective-permute-start | bytes 933896 | tf_op jit(solution)/shard_map/ppermute | solution.py:469
  37.0 0.0 collective-permute-done.17.got2
  37.1 2.6 %collective-permute-start.18 = (f32[168,256]{1,0:T(8,128)S(1)}, f32[168,256]{1,0:T(8,128)S(1)}, u32[]{:S(2)}, u32[]{:S(2)}) collective-permute-start(f32[168,256]{1,0:T(8,128)S(1)} %get-tuple-element.86.refs_2_), channel_id=1, source_target_pairs={{0,8},{4,12},{8,0},{12,4},{16,24},{20,28},{24,16},{28,20},{1,9},{5... | collective-permute-start | bytes 516104 | tf_op jit(solution)/shard_map/ppermute | solution.py:512
  39.7 0.0 collective-permute-done.11.pair2
  39.7 0.0 collective-permute-done.12.got1
  39.7 0.0 collective-permute-done.13.got2
  39.8 2.2 %collective-permute-start.14 = (f32[168,256]{1,0:T(8,128)S(1)}, f32[168,256]{1,0:T(8,128)S(1)}, u32[]{:S(2)}, u32[]{:S(2)}) collective-permute-start(f32[168,256]{1,0:T(8,128)S(1)} %get-tuple-element.79.refs_2_), channel_id=1, source_target_pairs={{0,8},{4,12},{8,0},{12,4},{16,24},{20,28},{24,16},{28,20},{1,9},{5... | collective-permute-start | bytes 516104 | tf_op jit(solution)/shard_map/ppermute | solution.py:512
  42.0 0.0 collective-permute-start.19
  42.0 0.5 %collective-permute-start.15 = (f32[152,256]{1,0:T(8,128)S(1)}, f32[152,256]{1,0:T(8,128)S(1)}, u32[]{:S(2)}, u32[]{:S(2)}) collective-permute-start(f32[152,256]{1,0:T(8,128)S(1)} %get-tuple-element.80), channel_id=1, source_target_pairs={{0,1},{1,0},{2,3},{3,2},{4,5},{5,4},{6,7},{7,6},{8,16},{9,17},{10,... | collective-permute-start | bytes 466952 | tf_op jit(solution)/shard_map/ppermute | solution.py:513
  42.5 0.9 %collective-permute-done.19.refs_4_ = f32[152,256]{1,0:T(8,128)S(1)} collective-permute-done((f32[152,256]{1,0:T(8,128)S(1)}, f32[152,256]{1,0:T(8,128)S(1)}, u32[]{:S(2)}, u32[]{:S(2)}) %collective-permute-start.19) | collective-permute-done | bytes 155680 | tf_op jit(solution)/shard_map/ppermute | solution.py:513
  43.4 1.6 %collective-permute-done.18.refs_3_ = f32[168,256]{1,0:T(8,128)S(1)} collective-permute-done((f32[168,256]{1,0:T(8,128)S(1)}, f32[168,256]{1,0:T(8,128)S(1)}, u32[]{:S(2)}, u32[]{:S(2)}) %collective-permute-start.18) | collective-permute-done | bytes 172064 | tf_op jit(solution)/shard_map/ppermute | solution.py:512
  45.0 0.2 collective-permute-done.7.refs_1_
  45.2 0.7 %last_ratio.2 = (f32[25,3072]{1,0:T(8,128)S(1)}, f32[1,25]{1,0:T(1,128)S(1)}) custom-call(f32[152,256]{1,0:T(8,128)S(1)} %get-tuple-element.82.refs_0_, f32[304,256]{1,0:T(8,128)S(1)} %collective-permute-done.7.refs_1_, f32[168,256]{1,0:T(8,128)S(1)} %get-tuple-element.86.refs_2_, f32[168,256]{1,0:T(8,128)S(1)} %collective-permute-done.18.refs_3_, ...), custom_call_target="tpu_custom_call" | custom-call | flops 1000 | tf_op jit(solution)/shard_map/last_ratio/pallas_call | solution.py:528
  45.9 0.0 collective-permute-done.15.refs_4_
  45.9 1.3 %collective-permute-done.14.refs_3_ = f32[168,256]{1,0:T(8,128)S(1)} collective-permute-done((f32[168,256]{1,0:T(8,128)S(1)}, f32[168,256]{1,0:T(8,128)S(1)}, u32[]{:S(2)}, u32[]{:S(2)}) %collective-permute-start.14) | collective-permute-done | bytes 172064 | tf_op jit(solution)/shard_map/ppermute | solution.py:512
  47.3 1.5 %last_ratio.3 = (f32[25,3072]{1,0:T(8,128)}, f32[25]{0:T(128)}) custom-call(f32[152,256]{1,0:T(8,128)S(1)} %get-tuple-element.55.refs_0_, f32[304,256]{1,0:T(8,128)S(1)} %collective-permute-done.7.refs_1_, f32[168,256]{1,0:T(8,128)S(1)} %get-tuple-element.79.refs_2_, f32[168,256]{1,0:T(8,128)S(1)} %collective-permute-done.14.refs_3_, ...), custom_call_target="tpu_custom_call" | custom-call | flops 1000 | tf_op jit(solution)/shard_map/last_ratio/pallas_call | solution.py:528
  (6 shorter events, 0.2 us)
Async XLA Ops:
  6.7 3.7 %collective-permute-start.2 = (f32[2,128]{1,0:T(2,128)S(1)}, f32[2,128]{1,0:T(2,128)S(1)}, u32[]{:S(2)}, u32[]{:S(2)}) collective-permute-start(f32[2,128]{1,0:T(2,128)S(1)} %get-tuple-element.48.refs_0_), channel_id=1, source_target_pairs={{0,3},{1,2},{2,1},{3,0},{4,7},{5,6},{6,5},{7,4},{8,11},{9,10},{10,... | collective-permute-start | bytes 3080 | tf_op jit(solution)/shard_map/ppermute | solution.py:606
  9.2 3.6 %collective-permute-start.1 = (f32[2,128]{1,0:T(2,128)S(1)}, f32[2,128]{1,0:T(2,128)S(1)}, u32[]{:S(2)}, u32[]{:S(2)}) collective-permute-start(f32[2,128]{1,0:T(2,128)S(1)} %get-tuple-element.48.refs_0_), channel_id=1, source_target_pairs={{0,2},{1,3},{2,0},{3,1},{4,6},{5,7},{6,4},{7,5},{8,10},{9,11},{10,... | collective-permute-start | bytes 3080 | tf_op jit(solution)/shard_map/ppermute | solution.py:606
  9.8 2.9 %collective-permute-start = (f32[2,128]{1,0:T(2,128)S(1)}, f32[2,128]{1,0:T(2,128)S(1)}, u32[]{:S(2)}, u32[]{:S(2)}) collective-permute-start(f32[2,128]{1,0:T(2,128)S(1)} %get-tuple-element.48.refs_0_), channel_id=1, source_target_pairs={{0,1},{1,0},{2,3},{3,2},{4,5},{5,4},{6,7},{7,6},{8,9},{9,8},{10,11... | collective-permute-start | bytes 3080 | tf_op jit(solution)/shard_map/ppermute | solution.py:606
  13.6 7.3 %collective-permute-start.3 = (f32[168,256]{1,0:T(8,128)S(1)}, f32[168,256]{1,0:T(8,128)S(1)}, u32[]{:S(2)}, u32[]{:S(2)}) collective-permute-start(f32[168,256]{1,0:T(8,128)S(1)} %get-tuple-element.53.send_a_ref), channel_id=1, source_target_pairs={{0,4},{4,0},{8,12},{12,8},{16,20},{20,16},{24,28},{28,24},{1,5},{5... | collective-permute-start | bytes 516104 | tf_op jit(solution)/shard_map/ppermute | solution.py:469
  15.4 8.7 %collective-permute-start.8 = (f32[168,256]{1,0:T(8,128)S(1)}, f32[168,256]{1,0:T(8,128)S(1)}, u32[]{:S(2)}, u32[]{:S(2)}) collective-permute-start(f32[168,256]{1,0:T(8,128)S(1)} %second_sums.1), channel_id=1, source_target_pairs={{0,4},{4,0},{8,12},{12,8},{16,20},{20,16},{24,28},{28,24},{1,5},{5... | collective-permute-start | bytes 516104 | tf_op jit(solution)/shard_map/ppermute | solution.py:469
  21.0 7.6 %collective-permute-start.5 = (f32[168,256]{1,0:T(8,128)S(1)}, f32[168,256]{1,0:T(8,128)S(1)}, u32[]{:S(2)}, u32[]{:S(2)}) collective-permute-start(f32[168,256]{1,0:T(8,128)S(1)} %join.6.sum0), channel_id=1, source_target_pairs={{0,8},{4,12},{8,0},{12,4},{16,24},{20,28},{24,16},{28,20},{1,9},{5... | collective-permute-start | bytes 516104 | tf_op jit(solution)/shard_map/ppermute | solution.py:503
  22.6 6.0 %collective-permute-start.4 = (f32[152,256]{1,0:T(8,128)S(1)}, f32[152,256]{1,0:T(8,128)S(1)}, u32[]{:S(2)}, u32[]{:S(2)}) collective-permute-start(f32[152,256]{1,0:T(8,128)S(1)} %get-tuple-element.61), channel_id=1, source_target_pairs={{0,4},{4,0},{8,12},{12,8},{16,20},{20,16},{24,28},{28,24},{1,5},{5... | collective-permute-start | bytes 466952 | tf_op jit(solution)/shard_map/ppermute | solution.py:469
  24.2 7.5 %collective-permute-start.9 = (f32[152,256]{1,0:T(8,128)S(1)}, f32[152,256]{1,0:T(8,128)S(1)}, u32[]{:S(2)}, u32[]{:S(2)}) collective-permute-start(f32[152,256]{1,0:T(8,128)S(1)} %get-tuple-element.72), channel_id=1, source_target_pairs={{0,4},{4,0},{8,12},{12,8},{16,20},{20,16},{24,28},{28,24},{1,5},{5... | collective-permute-start | bytes 466952 | tf_op jit(solution)/shard_map/ppermute | solution.py:469
  25.8 6.6 %collective-permute-start.10 = (f32[168,256]{1,0:T(8,128)S(1)}, f32[168,256]{1,0:T(8,128)S(1)}, u32[]{:S(2)}, u32[]{:S(2)}) collective-permute-start(f32[168,256]{1,0:T(8,128)S(1)} %join.8.sum0), channel_id=1, source_target_pairs={{0,8},{4,12},{8,0},{12,4},{16,24},{20,28},{24,16},{28,20},{1,9},{5... | collective-permute-start | bytes 516104 | tf_op jit(solution)/shard_map/ppermute | solution.py:503
  28.6 6.8 %collective-permute-start.6 = (f32[152,256]{1,0:T(8,128)S(1)}, f32[152,256]{1,0:T(8,128)S(1)}, u32[]{:S(2)}, u32[]{:S(2)}) collective-permute-start(f32[152,256]{1,0:T(8,128)S(1)} %get-tuple-element.65), channel_id=1, source_target_pairs={{0,4},{4,0},{8,12},{12,8},{16,20},{20,16},{24,28},{28,24},{1,5},{5... | collective-permute-start | bytes 466952 | tf_op jit(solution)/shard_map/ppermute | solution.py:469
  30.2 5.7 %collective-permute-start.16 = (f32[152,256]{1,0:T(8,128)S(1)}, f32[152,256]{1,0:T(8,128)S(1)}, u32[]{:S(2)}, u32[]{:S(2)}) collective-permute-start(f32[152,256]{1,0:T(8,128)S(1)} %get-tuple-element.84.sum1), channel_id=1, source_target_pairs={{0,8},{4,12},{8,0},{12,4},{16,24},{20,28},{24,16},{28,20},{1,9},{5... | collective-permute-start | bytes 466952 | tf_op jit(solution)/shard_map/ppermute | solution.py:507
  31.7 5.4 %collective-permute-start.17 = (f32[168,256]{1,0:T(8,128)S(1)}, f32[168,256]{1,0:T(8,128)S(1)}, u32[]{:S(2)}, u32[]{:S(2)}) collective-permute-start(f32[168,256]{1,0:T(8,128)S(1)} %get-tuple-element.85.both0), channel_id=1, source_target_pairs={{0,1},{1,0},{2,3},{3,2},{4,5},{5,4},{6,7},{7,6},{8,16},{9,17},{10,... | collective-permute-start | bytes 516104 | tf_op jit(solution)/shard_map/ppermute | solution.py:508
  32.4 7.3 %collective-permute-start.11 = (f32[152,256]{1,0:T(8,128)S(1)}, f32[152,256]{1,0:T(8,128)S(1)}, u32[]{:S(2)}, u32[]{:S(2)}) collective-permute-start(f32[152,256]{1,0:T(8,128)S(1)} %get-tuple-element.76), channel_id=1, source_target_pairs={{0,4},{4,0},{8,12},{12,8},{16,20},{20,16},{24,28},{28,24},{1,5},{5... | collective-permute-start | bytes 466952 | tf_op jit(solution)/shard_map/ppermute | solution.py:469
  33.4 6.3 %collective-permute-start.12 = (f32[152,256]{1,0:T(8,128)S(1)}, f32[152,256]{1,0:T(8,128)S(1)}, u32[]{:S(2)}, u32[]{:S(2)}) collective-permute-start(f32[152,256]{1,0:T(8,128)S(1)} %get-tuple-element.77.sum1), channel_id=1, source_target_pairs={{0,8},{4,12},{8,0},{12,4},{16,24},{20,28},{24,16},{28,20},{1,9},{5... | collective-permute-start | bytes 466952 | tf_op jit(solution)/shard_map/ppermute | solution.py:507
  35.4 4.3 %collective-permute-start.13 = (f32[168,256]{1,0:T(8,128)S(1)}, f32[168,256]{1,0:T(8,128)S(1)}, u32[]{:S(2)}, u32[]{:S(2)}) collective-permute-start(f32[168,256]{1,0:T(8,128)S(1)} %get-tuple-element.78.both0), channel_id=1, source_target_pairs={{0,1},{1,0},{2,3},{3,2},{4,5},{5,4},{6,7},{7,6},{8,16},{9,17},{10,... | collective-permute-start | bytes 516104 | tf_op jit(solution)/shard_map/ppermute | solution.py:508
  35.9 9.3 %collective-permute-start.7 = (f32[304,256]{1,0:T(8,128)S(1)}, f32[304,256]{1,0:T(8,128)S(1)}, u32[]{:S(2)}, u32[]{:S(2)}) collective-permute-start(f32[304,256]{1,0:T(8,128)S(1)} %get-tuple-element.66), channel_id=1, source_target_pairs={{0,4},{4,0},{8,12},{12,8},{16,20},{20,16},{24,28},{28,24},{1,5},{5... | collective-permute-start | bytes 933896 | tf_op jit(solution)/shard_map/ppermute | solution.py:469
  37.1 7.9 %collective-permute-start.18 = (f32[168,256]{1,0:T(8,128)S(1)}, f32[168,256]{1,0:T(8,128)S(1)}, u32[]{:S(2)}, u32[]{:S(2)}) collective-permute-start(f32[168,256]{1,0:T(8,128)S(1)} %get-tuple-element.86.refs_2_), channel_id=1, source_target_pairs={{0,8},{4,12},{8,0},{12,4},{16,24},{20,28},{24,16},{28,20},{1,9},{5... | collective-permute-start | bytes 516104 | tf_op jit(solution)/shard_map/ppermute | solution.py:512
  39.8 7.5 %collective-permute-start.14 = (f32[168,256]{1,0:T(8,128)S(1)}, f32[168,256]{1,0:T(8,128)S(1)}, u32[]{:S(2)}, u32[]{:S(2)}) collective-permute-start(f32[168,256]{1,0:T(8,128)S(1)} %get-tuple-element.79.refs_2_), channel_id=1, source_target_pairs={{0,8},{4,12},{8,0},{12,4},{16,24},{20,28},{24,16},{28,20},{1,9},{5... | collective-permute-start | bytes 516104 | tf_op jit(solution)/shard_map/ppermute | solution.py:512
  42.0 1.4 %collective-permute-start.19 = (f32[152,256]{1,0:T(8,128)S(1)}, f32[152,256]{1,0:T(8,128)S(1)}, u32[]{:S(2)}, u32[]{:S(2)}) collective-permute-start(f32[152,256]{1,0:T(8,128)S(1)} %get-tuple-element.87), channel_id=1, source_target_pairs={{0,1},{1,0},{2,3},{3,2},{4,5},{5,4},{6,7},{7,6},{8,16},{9,17},{10,... | collective-permute-start | bytes 466952 | tf_op jit(solution)/shard_map/ppermute | solution.py:513
  42.0 3.9 %collective-permute-start.15 = (f32[152,256]{1,0:T(8,128)S(1)}, f32[152,256]{1,0:T(8,128)S(1)}, u32[]{:S(2)}, u32[]{:S(2)}) collective-permute-start(f32[152,256]{1,0:T(8,128)S(1)} %get-tuple-element.80), channel_id=1, source_target_pairs={{0,1},{1,0},{2,3},{3,2},{4,5},{5,4},{6,7},{7,6},{8,16},{9,17},{10,... | collective-permute-start | bytes 466952 | tf_op jit(solution)/shard_map/ppermute | solution.py:513

commit v4 on v3

--- a/solution.py
+++ b/solution.py
@@ -141,12 +141,13 @@
 
     flat_bf_ref[...] = flat_ref[...].astype(BF16)
     total = nshift * count
-    pairs = [list(range(s, min(s + 4, nshift))) for s in range(0, nshift, 4)]
+    part = -(-nshift // 2)
+    parts = [list(range(s, min(s + part, nshift))) for s in range(0, nshift, part)]
     peak = None
-    build(pairs[0])
-    for index, shifts in enumerate(pairs):
-        if index + 1 < len(pairs):
-            build(pairs[index + 1])
+    build(parts[0])
+    for index, shifts in enumerate(parts):
+        if index + 1 < len(parts):
+            build(parts[index + 1])
         at = shifts[0] * count
         cross = lax.dot_general(
             flat_bf_ref[...], copies_ref[at : at + len(shifts) * count, :], (((1,), (1,)), ((), ())),
@@ -215,8 +216,7 @@
     )
 
 
-def posterior(stats_refs, weight_ref, onehot_ref, post_ref, loglik_ref):
-    count = onehot_ref.shape[1]
+def normaliser(stats_refs):
     parts = len(stats_refs)
     me = lax.axis_index("cls")
     stats = [ref[...] for ref in stats_refs]
@@ -233,23 +233,21 @@
     for value in ordered:
         total = total + value[1:2] * jnp.exp(value[0:1] - peak)
     loglik = peak + jnp.log(total)
-    scale = jnp.exp(stats[0][0:1] - loglik)
-    loglik_ref[...] = loglik.reshape(count)
+    return loglik, jnp.exp(stats[0][0:1] - loglik)
+
+
+def posterior(weight_ref, rows, scale, onehot_ref, post_ref):
+    count = onehot_ref.shape[1]
     per_img = None
     for at in range(0, weight_ref.shape[1], count):
-        post = (weight_ref[:, at : at + count] * scale).astype(BF16)
-        post_ref[:, at : at + count] = post
+        post = (weight_ref[rows, at : at + count] * scale).astype(BF16)
+        post_ref[rows, at : at + count] = post
         post = post.astype(F32)
         per_img = post if per_img is None else per_img + post
     three = jnp.concatenate([onehot_ref[...]] * 3, axis=1).astype(BF16)
-    hpad = per_img.shape[0] // 2
-    return [
-        lax.dot_general(
-            three, thirds(per_img[at : at + hpad], 1), (((1,), (1,)), ((), ())),
-            preferred_element_type=F32,
-        )
-        for at in (0, hpad)
-    ]
+    return lax.dot_general(
+        three, thirds(per_img, 1), (((1,), (1,)), ((), ())), preferred_element_type=F32
+    )
 
 
 def class_sums(post_ref, copies_ref, rows, at, width):
@@ -258,7 +256,7 @@
 
 LINE = 4
 PAIR = 2
-SLOW = 4_000_000_000
+SLOW = 2_000_000_000
 QUICK = 1000
 
 
@@ -283,25 +281,33 @@
 
 def first_kernel(nstat, *refs):
     stats_refs = refs[:nstat]
-    weight_ref, copies_ref, onehot_ref, post_ref, send_ref, mass_ref, loglik_ref = refs[nstat:]
-    hpad = post_ref.shape[0] // 2
-    ngroup = onehot_ref.shape[0]
+    weight_ref, copies_ref, onehot_ref, post_ref, send_ref, scale_ref, loglik_ref = refs[nstat:]
+    hpad = post_ref.shape[0]
     width = send_ref.shape[1]
-    send = send_ref.shape[0] - ngroup
-    mass = posterior(stats_refs, weight_ref, onehot_ref, post_ref, loglik_ref)
-    sums = class_sums(post_ref, copies_ref, pl.ds(0, hpad), owner_column(0, False, width), width)
+    send = send_ref.shape[0] - onehot_ref.shape[0]
+    rows = pl.ds(0, hpad)
+    loglik, scale = normaliser(stats_refs)
+    loglik_ref[...] = loglik.reshape(loglik.shape[1])
+    scale_ref[...] = scale
+    mass = posterior(weight_ref, rows, scale, onehot_ref, post_ref)
+    sums = class_sums(post_ref, copies_ref, rows, owner_column(0, False, width), width)
     send_ref[0:send, :] = sums[0:send]
-    put_mass(send_ref, mass[0])
-    put_mass(mass_ref, mass[1])
-
-
-def second_kernel(post_ref, copies_ref, mass_ref, send_ref):
+    put_mass(send_ref, mass)
+
+
+def second_kernel(
+    first_ref, scale_ref, weight_ref, copies_ref, onehot_ref, post_ref, send_ref, mass_ref
+):
     hpad = post_ref.shape[0] // 2
     width = send_ref.shape[1]
-    send = send_ref.shape[0] - mass_ref.shape[0]
-    sums = class_sums(post_ref, copies_ref, pl.ds(hpad, hpad), owner_column(0, False, width), width)
+    send = send_ref.shape[0] - onehot_ref.shape[0]
+    rows = pl.ds(hpad, hpad)
+    mass = posterior(weight_ref, rows, scale_ref[...], onehot_ref, post_ref)
+    sums = class_sums(post_ref, copies_ref, rows, owner_column(0, False, width), width)
     send_ref[0:send, :] = sums[0:send]
-    send_ref[send:, :] = mass_ref[...]
+    put_mass(send_ref, mass)
+    put_mass(mass_ref, mass)
+    post_ref[0:hpad, :] = first_ref[...]
 
 
 def rest_kernel(post_ref, copies_ref, send_a_ref, mass_ref, *out_refs):
@@ -419,27 +425,29 @@
     def first(*refs):
         first_kernel(len(stats), *refs)
 
-    post, send_a, mass_b, loglik = pl.pallas_call(
+    rpad, total = weight.shape
+    count = onehot.shape[1]
+    post_a, send_a, scale, loglik = pl.pallas_call(
         first,
         out_shape=(
-            jax.ShapeDtypeStruct(weight.shape, BF16),
+            jax.ShapeDtypeStruct((rpad // 2, total), BF16),
             full,
-            mass_shape,
-            jax.ShapeDtypeStruct(onehot.shape[1:], F32),
+            jax.ShapeDtypeStruct((1, count), F32),
+            jax.ShapeDtypeStruct((count,), F32),
         ),
         in_specs=[VMEM] * (len(stats) + 3),
         out_specs=(VMEM,) * 4,
         compiler_params=PARAMS,
         name="first_sums",
     )(*stats, weight, copies, onehot)
-    send_b = pl.pallas_call(
+    post, send_b, mass_b = pl.pallas_call(
         second_kernel,
-        out_shape=full,
-        in_specs=[VMEM] * 3,
-        out_specs=VMEM,
+        out_shape=(jax.ShapeDtypeStruct(weight.shape, BF16), full, mass_shape),
+        in_specs=[VMEM] * 5,
+        out_specs=(VMEM,) * 3,
         compiler_params=PARAMS,
         name="second_sums",
-    )(post, copies, mass_b)
+    )(post_a, scale, weight, copies, onehot)
     parts = pl.pallas_call(
         rest_kernel,
         out_shape=((full,) + (body,) * 5) * 2 + (jax.ShapeDtypeStruct((2 * send, width), F32),),
@@ -553,9 +561,11 @@
 
     def sums(*refs):
         weight_ref, copies_ref, onehot_ref, num_ref, mass_ref, loglik_ref, post_ref = refs[nstat:]
-        mass = posterior(refs[:nstat], weight_ref, onehot_ref, post_ref, loglik_ref)
-        mass_ref[0] = mass[0]
-        mass_ref[1] = mass[1]
+        loglik, scale = normaliser(refs[:nstat])
+        loglik_ref[...] = loglik.reshape(loglik.shape[1])
+        for index in range(2):
+            rows = pl.ds(index * hpad, hpad)
+            mass_ref[index] = posterior(weight_ref, rows, scale, onehot_ref, post_ref)
         for at in range(0, two_f, 256):
             num_ref[:, at : at + 256] = class_sums(
                 post_ref, copies_ref, pl.ds(0, rpad), at, 256

time: 48.9 us -> 48.6 us (level)
  no operation moved by 1% of the time
where the time goes in v4:
time: 48.6 us; the launch traced here: 48.5 us
  starting transfers between devices  24.6 us (51%)
  Pallas kernels  12.2 us (25%)
  waiting for transfers between devices  11 us (23%)
  between operations  0.72 us (1%)
    ppermute x7, starting transfers between devices, swap(): return lax.ppermute(value, 'dom', across)  8.91 us
    pallas_call x1, Pallas kernels, estep(): pl.pallas_call(estep_kernel, out_shape=(jax.ShapeDtypeStruct((rpad, nshif...  5.86 us
    ppermute x2, starting transfers between devices, reduce_chain(): line = lax.ppermute(to_ends, 'dom', outer)  4.87 us
    ppermute x2, starting transfers between devices, reduce_chain(): got0 = lax.ppermute(sum0, 'dom', outer)  3.69 us
    ppermute x2, starting transfers between devices, reduce_chain(): got1 = lax.ppermute(sum1, 'dom', outer)  3.45 us
    ppermute x7, waiting for transfers between devices, swap(): return lax.ppermute(value, 'dom', across)  3.14 us
    ppermute x3, starting transfers between devices, local(): lax.ppermute(stat, 'cls', [(c, c ^ other) for c in range(cls_n)])  3.12 us
    ppermute x2, waiting for transfers between devices, reduce_chain(): line = lax.ppermute(to_ends, 'dom', outer)  2.92 us
  transfers between devices with their start and end apart: 20, of which 10 were waited for; matrix products, arithmetic and copies ran while one was open for 0% of the time, Pallas kernels for 8%

profile of v4, /device:TPU:0, one launch (start us, length us, event | category | flops | bytes accessed | tf_op | source)
XLA Modules:
  0.0 48.5 jit_solution(15013278235255715682)
XLA Ops:
  0.6 5.9 %estep.1 = (f32[320,1152]{1,0:T(8,128)S(1)}, bf16[1152,2048]{1,0:T(8,128)(2,1)S(1)}, f32[2,128]{1,0:T(2,128)S(1)}, f32[16,128]{1,0:T(8,128)S(1)}, f32[16,256]{1,0:T(8,128)S(1)}) custom-call(bf16[128,2048]{1,0:T(8,128)(2,1)} %images_hbm.1, bf16[12,25,2048]{2,1,0:T(8,128)(2,1)} %bitcast.2, f32[16,1024]{1,0:T(8,128)} %ctf_hbm.1, f32[16,1024]{1,0:T(8,128)} %inv_hbm.1, ...), custom_call_target="tpu_custom_call" | custom-call | tf_op jit(solution)/shard_map/estep/pallas_call | solution.py:182
  6.5 2.4 %collective-permute-start.2 = (f32[2,128]{1,0:T(2,128)S(1)}, f32[2,128]{1,0:T(2,128)S(1)}, u32[]{:S(2)}, u32[]{:S(2)}) collective-permute-start(f32[2,128]{1,0:T(2,128)S(1)} %get-tuple-element.51.refs_0_), channel_id=1, source_target_pairs={{0,3},{1,2},{2,1},{3,0},{4,7},{5,6},{6,5},{7,4},{8,11},{9,10},{10,... | collective-permute-start | bytes 3080 | tf_op jit(solution)/shard_map/ppermute | solution.py:616
  8.9 0.6 %collective-permute-start.1 = (f32[2,128]{1,0:T(2,128)S(1)}, f32[2,128]{1,0:T(2,128)S(1)}, u32[]{:S(2)}, u32[]{:S(2)}) collective-permute-start(f32[2,128]{1,0:T(2,128)S(1)} %get-tuple-element.51.refs_0_), channel_id=1, source_target_pairs={{0,2},{1,3},{2,0},{3,1},{4,6},{5,7},{6,4},{7,5},{8,10},{9,11},{10,... | collective-permute-start | bytes 3080 | tf_op jit(solution)/shard_map/ppermute | solution.py:616
  9.6 0.0 collective-permute-start
  9.6 0.6 %collective-permute-done.2.refs_3_ = f32[2,128]{1,0:T(2,128)S(1)} collective-permute-done((f32[2,128]{1,0:T(2,128)S(1)}, f32[2,128]{1,0:T(2,128)S(1)}, u32[]{:S(2)}, u32[]{:S(2)}) %collective-permute-start.2) | collective-permute-done | bytes 1056 | tf_op jit(solution)/shard_map/ppermute | solution.py:616
  10.2 2.3 %collective-permute-done.1.refs_2_ = f32[2,128]{1,0:T(2,128)S(1)} collective-permute-done((f32[2,128]{1,0:T(2,128)S(1)}, f32[2,128]{1,0:T(2,128)S(1)}, u32[]{:S(2)}, u32[]{:S(2)}) %collective-permute-start.1) | collective-permute-done | bytes 1056 | tf_op jit(solution)/shard_map/ppermute | solution.py:616
  12.5 0.0 collective-permute-done.refs_1_
  12.5 0.8 %first_sums.1 = (bf16[160,1152]{1,0:T(8,128)(2,1)S(1)}, f32[168,256]{1,0:T(8,128)S(1)}, f32[1,128]{1,0:T(1,128)S(1)}, f32[128]{0:T(128)}) custom-call(f32[2,128]{1,0:T(2,128)S(1)} %get-tuple-element.51.refs_0_, f32[2,128]{1,0:T(2,128)S(1)} %collective-permute-done.refs_1_, f32[2,128]{1,0:T(2,128)S(1)} %collective-permute-done.1.refs_2_, ...), custom_call_target="tpu_custom_call" | custom-call | tf_op jit(solution)/shard_map/first_sums/pallas_call | solution.py:430
  13.3 1.5 %collective-permute-start.3 = (f32[168,256]{1,0:T(8,128)S(1)}, f32[168,256]{1,0:T(8,128)S(1)}, u32[]{:S(2)}, u32[]{:S(2)}) collective-permute-start(f32[168,256]{1,0:T(8,128)S(1)} %get-tuple-element.58.send_a_ref), channel_id=1, source_target_pairs={{0,4},{4,0},{8,12},{12,8},{16,20},{20,16},{24,28},{28,24},{1,5},{5... | collective-permute-start | bytes 516104 | tf_op jit(solution)/shard_map/ppermute | solution.py:477
  14.9 0.4 second_sums.1
  15.3 0.6 %collective-permute-start.8 = (f32[168,256]{1,0:T(8,128)S(1)}, f32[168,256]{1,0:T(8,128)S(1)}, u32[]{:S(2)}, u32[]{:S(2)}) collective-permute-start(f32[168,256]{1,0:T(8,128)S(1)} %get-tuple-element.77), channel_id=1, source_target_pairs={{0,4},{4,0},{8,12},{12,8},{16,20},{20,16},{24,28},{28,24},{1,5},{5... | collective-permute-start | bytes 516104 | tf_op jit(solution)/shard_map/ppermute | solution.py:477
  15.9 2.7 %rest_sums.1 = (f32[168,256]{1,0:T(8,128)S(1)}, f32[152,256]{1,0:T(8,128)S(1)}, f32[152,256]{1,0:T(8,128)S(1)}, f32[152,256]{1,0:T(8,128)S(1)}, f32[152,256]{1,0...) custom-call(bf16[320,1152]{1,0:T(8,128)(2,1)S(1)} %get-tuple-element, ...), custom_call_target="tpu_custom_call" | custom-call | tf_op jit(solution)/shard_map/rest_sums/pallas_call | solution.py:451
  18.6 2.1 %collective-permute-done.3.right = f32[168,256]{1,0:T(8,128)S(1)} collective-permute-done((f32[168,256]{1,0:T(8,128)S(1)}, f32[168,256]{1,0:T(8,128)S(1)}, u32[]{:S(2)}, u32[]{:S(2)}) %collective-permute-start.3) | collective-permute-done | bytes 172064 | tf_op jit(solution)/shard_map/ppermute | solution.py:477
  20.7 1.6 %collective-permute-start.5 = (f32[168,256]{1,0:T(8,128)S(1)}, f32[168,256]{1,0:T(8,128)S(1)}, u32[]{:S(2)}, u32[]{:S(2)}) collective-permute-start(f32[168,256]{1,0:T(8,128)S(1)} %join.6.sum0), channel_id=1, source_target_pairs={{0,8},{4,12},{8,0},{12,4},{16,24},{20,28},{24,16},{28,20},{1,9},{5... | collective-permute-start | bytes 516104 | tf_op jit(solution)/shard_map/ppermute | solution.py:511
  22.3 1.5 %collective-permute-start.4 = (f32[152,256]{1,0:T(8,128)S(1)}, f32[152,256]{1,0:T(8,128)S(1)}, u32[]{:S(2)}, u32[]{:S(2)}) collective-permute-start(f32[152,256]{1,0:T(8,128)S(1)} %get-tuple-element.66), channel_id=1, source_target_pairs={{0,4},{4,0},{8,12},{12,8},{16,20},{20,16},{24,28},{28,24},{1,5},{5... | collective-permute-start | bytes 466952 | tf_op jit(solution)/shard_map/ppermute | solution.py:477
  23.8 0.0 collective-permute-done.8.right
  23.9 1.6 %collective-permute-start.9 = (f32[152,256]{1,0:T(8,128)S(1)}, f32[152,256]{1,0:T(8,128)S(1)}, u32[]{:S(2)}, u32[]{:S(2)}) collective-permute-start(f32[152,256]{1,0:T(8,128)S(1)} %get-tuple-element.78), channel_id=1, source_target_pairs={{0,4},{4,0},{8,12},{12,8},{16,20},{20,16},{24,28},{28,24},{1,5},{5... | collective-permute-start | bytes 466952 | tf_op jit(solution)/shard_map/ppermute | solution.py:477
  25.5 2.0 %collective-permute-start.10 = (f32[168,256]{1,0:T(8,128)S(1)}, f32[168,256]{1,0:T(8,128)S(1)}, u32[]{:S(2)}, u32[]{:S(2)}) collective-permute-start(f32[168,256]{1,0:T(8,128)S(1)} %join.8.sum0), channel_id=1, source_target_pairs={{0,8},{4,12},{8,0},{12,4},{16,24},{20,28},{24,16},{28,20},{1,9},{5... | collective-permute-start | bytes 516104 | tf_op jit(solution)/shard_map/ppermute | solution.py:511
  27.5 0.8 %collective-permute-done.4.pair1 = f32[152,256]{1,0:T(8,128)S(1)} collective-permute-done((f32[152,256]{1,0:T(8,128)S(1)}, f32[152,256]{1,0:T(8,128)S(1)}, u32[]{:S(2)}, u32[]{:S(2)}) %collective-permute-start.4) | collective-permute-done | bytes 155680 | tf_op jit(solution)/shard_map/ppermute | solution.py:477
  28.3 0.0 collective-permute-done.5.got0
  28.3 1.6 %collective-permute-start.6 = (f32[152,256]{1,0:T(8,128)S(1)}, f32[152,256]{1,0:T(8,128)S(1)}, u32[]{:S(2)}, u32[]{:S(2)}) collective-permute-start(f32[152,256]{1,0:T(8,128)S(1)} %get-tuple-element.70), channel_id=1, source_target_pairs={{0,4},{4,0},{8,12},{12,8},{16,20},{20,16},{24,28},{28,24},{1,5},{5... | collective-permute-start | bytes 466952 | tf_op jit(solution)/shard_map/ppermute | solution.py:477
  29.9 1.4 %collective-permute-start.16 = (f32[152,256]{1,0:T(8,128)S(1)}, f32[152,256]{1,0:T(8,128)S(1)}, u32[]{:S(2)}, u32[]{:S(2)}) collective-permute-start(f32[152,256]{1,0:T(8,128)S(1)} %get-tuple-element.90.sum1), channel_id=1, source_target_pairs={{0,8},{4,12},{8,0},{12,4},{16,24},{20,28},{24,16},{28,20},{1,9},{5... | collective-permute-start | bytes 466952 | tf_op jit(solution)/shard_map/ppermute | solution.py:515
  31.4 0.0 collective-permute-start.17
  31.4 0.0 collective-permute-done.9.pair1
  31.4 0.7 %collective-permute-done.10.got0 = f32[168,256]{1,0:T(8,128)S(1)} collective-permute-done((f32[168,256]{1,0:T(8,128)S(1)}, f32[168,256]{1,0:T(8,128)S(1)}, u32[]{:S(2)}, u32[]{:S(2)}) %collective-permute-start.10) | collective-permute-done | bytes 172064 | tf_op jit(solution)/shard_map/ppermute | solution.py:511
  32.1 1.0 %collective-permute-start.11 = (f32[152,256]{1,0:T(8,128)S(1)}, f32[152,256]{1,0:T(8,128)S(1)}, u32[]{:S(2)}, u32[]{:S(2)}) collective-permute-start(f32[152,256]{1,0:T(8,128)S(1)} %get-tuple-element.82), channel_id=1, source_target_pairs={{0,4},{4,0},{8,12},{12,8},{16,20},{20,16},{24,28},{28,24},{1,5},{5... | collective-permute-start | bytes 466952 | tf_op jit(solution)/shard_map/ppermute | solution.py:477
  33.1 2.0 %collective-permute-start.12 = (f32[152,256]{1,0:T(8,128)S(1)}, f32[152,256]{1,0:T(8,128)S(1)}, u32[]{:S(2)}, u32[]{:S(2)}) collective-permute-start(f32[152,256]{1,0:T(8,128)S(1)} %get-tuple-element.83.sum1), channel_id=1, source_target_pairs={{0,8},{4,12},{8,0},{12,4},{16,24},{20,28},{24,16},{28,20},{1,9},{5... | collective-permute-start | bytes 466952 | tf_op jit(solution)/shard_map/ppermute | solution.py:515
  35.1 0.0 collective-permute-done.6.pair2
  35.1 0.0 collective-permute-start.13
  35.1 0.4 collective-permute-done.16.got1
  35.6 1.1 %collective-permute-start.7 = (f32[304,256]{1,0:T(8,128)S(1)}, f32[304,256]{1,0:T(8,128)S(1)}, u32[]{:S(2)}, u32[]{:S(2)}) collective-permute-start(f32[304,256]{1,0:T(8,128)S(1)} %get-tuple-element.71), channel_id=1, source_target_pairs={{0,4},{4,0},{8,12},{12,8},{16,20},{20,16},{24,28},{28,24},{1,5},{5... | collective-permute-start | bytes 933896 | tf_op jit(solution)/shard_map/ppermute | solution.py:477
  36.7 0.0 collective-permute-done.17.got2
  36.8 2.6 %collective-permute-start.18 = (f32[168,256]{1,0:T(8,128)S(1)}, f32[168,256]{1,0:T(8,128)S(1)}, u32[]{:S(2)}, u32[]{:S(2)}) collective-permute-start(f32[168,256]{1,0:T(8,128)S(1)} %get-tuple-element.92.refs_2_), channel_id=1, source_target_pairs={{0,8},{4,12},{8,0},{12,4},{16,24},{20,28},{24,16},{28,20},{1,9},{5... | collective-permute-start | bytes 516104 | tf_op jit(solution)/shard_map/ppermute | solution.py:520
  39.4 0.0 collective-permute-done.11.pair2
  39.4 0.0 collective-permute-done.12.got1
  39.4 0.0 collective-permute-done.13.got2
  39.5 2.2 %collective-permute-start.14 = (f32[168,256]{1,0:T(8,128)S(1)}, f32[168,256]{1,0:T(8,128)S(1)}, u32[]{:S(2)}, u32[]{:S(2)}) collective-permute-start(f32[168,256]{1,0:T(8,128)S(1)} %get-tuple-element.85.refs_2_), channel_id=1, source_target_pairs={{0,8},{4,12},{8,0},{12,4},{16,24},{20,28},{24,16},{28,20},{1,9},{5... | collective-permute-start | bytes 516104 | tf_op jit(solution)/shard_map/ppermute | solution.py:520
  41.7 0.0 collective-permute-start.19
  41.7 0.5 %collective-permute-start.15 = (f32[152,256]{1,0:T(8,128)S(1)}, f32[152,256]{1,0:T(8,128)S(1)}, u32[]{:S(2)}, u32[]{:S(2)}) collective-permute-start(f32[152,256]{1,0:T(8,128)S(1)} %get-tuple-element.86), channel_id=1, source_target_pairs={{0,1},{1,0},{2,3},{3,2},{4,5},{5,4},{6,7},{7,6},{8,16},{9,17},{10,... | collective-permute-start | bytes 466952 | tf_op jit(solution)/shard_map/ppermute | solution.py:521
  42.2 0.9 %collective-permute-done.19.refs_4_ = f32[152,256]{1,0:T(8,128)S(1)} collective-permute-done((f32[152,256]{1,0:T(8,128)S(1)}, f32[152,256]{1,0:T(8,128)S(1)}, u32[]{:S(2)}, u32[]{:S(2)}) %collective-permute-start.19) | collective-permute-done | bytes 155680 | tf_op jit(solution)/shard_map/ppermute | solution.py:521
  43.1 1.6 %collective-permute-done.18.refs_3_ = f32[168,256]{1,0:T(8,128)S(1)} collective-permute-done((f32[168,256]{1,0:T(8,128)S(1)}, f32[168,256]{1,0:T(8,128)S(1)}, u32[]{:S(2)}, u32[]{:S(2)}) %collective-permute-start.18) | collective-permute-done | bytes 172064 | tf_op jit(solution)/shard_map/ppermute | solution.py:520
  44.7 0.2 collective-permute-done.7.refs_1_
  44.9 0.7 %last_ratio.2 = (f32[25,3072]{1,0:T(8,128)S(1)}, f32[1,25]{1,0:T(1,128)S(1)}) custom-call(f32[152,256]{1,0:T(8,128)S(1)} %get-tuple-element.88.refs_0_, f32[304,256]{1,0:T(8,128)S(1)} %collective-permute-done.7.refs_1_, f32[168,256]{1,0:T(8,128)S(1)} %get-tuple-element.92.refs_2_, f32[168,256]{1,0:T(8,128)S(1)} %collective-permute-done.18.refs_3_, ...), custom_call_target="tpu_custom_call" | custom-call | flops 1000 | tf_op jit(solution)/shard_map/last_ratio/pallas_call | solution.py:536
  45.6 0.0 collective-permute-done.15.refs_4_
  45.7 1.3 %collective-permute-done.14.refs_3_ = f32[168,256]{1,0:T(8,128)S(1)} collective-permute-done((f32[168,256]{1,0:T(8,128)S(1)}, f32[168,256]{1,0:T(8,128)S(1)}, u32[]{:S(2)}, u32[]{:S(2)}) %collective-permute-start.14) | collective-permute-done | bytes 172064 | tf_op jit(solution)/shard_map/ppermute | solution.py:520
  47.0 1.5 %last_ratio.3 = (f32[25,3072]{1,0:T(8,128)}, f32[25]{0:T(128)}) custom-call(f32[152,256]{1,0:T(8,128)S(1)} %get-tuple-element.60.refs_0_, f32[304,256]{1,0:T(8,128)S(1)} %collective-permute-done.7.refs_1_, f32[168,256]{1,0:T(8,128)S(1)} %get-tuple-element.85.refs_2_, f32[168,256]{1,0:T(8,128)S(1)} %collective-permute-done.14.refs_3_, ...), custom_call_target="tpu_custom_call" | custom-call | flops 1000 | tf_op jit(solution)/shard_map/last_ratio/pallas_call | solution.py:536
  (6 shorter events, 0.2 us)
Async XLA Ops:
  6.5 3.7 %collective-permute-start.2 = (f32[2,128]{1,0:T(2,128)S(1)}, f32[2,128]{1,0:T(2,128)S(1)}, u32[]{:S(2)}, u32[]{:S(2)}) collective-permute-start(f32[2,128]{1,0:T(2,128)S(1)} %get-tuple-element.51.refs_0_), channel_id=1, source_target_pairs={{0,3},{1,2},{2,1},{3,0},{4,7},{5,6},{6,5},{7,4},{8,11},{9,10},{10,... | collective-permute-start | bytes 3080 | tf_op jit(solution)/shard_map/ppermute | solution.py:616
  8.9 3.6 %collective-permute-start.1 = (f32[2,128]{1,0:T(2,128)S(1)}, f32[2,128]{1,0:T(2,128)S(1)}, u32[]{:S(2)}, u32[]{:S(2)}) collective-permute-start(f32[2,128]{1,0:T(2,128)S(1)} %get-tuple-element.51.refs_0_), channel_id=1, source_target_pairs={{0,2},{1,3},{2,0},{3,1},{4,6},{5,7},{6,4},{7,5},{8,10},{9,11},{10,... | collective-permute-start | bytes 3080 | tf_op jit(solution)/shard_map/ppermute | solution.py:616
  9.6 2.9 %collective-permute-start = (f32[2,128]{1,0:T(2,128)S(1)}, f32[2,128]{1,0:T(2,128)S(1)}, u32[]{:S(2)}, u32[]{:S(2)}) collective-permute-start(f32[2,128]{1,0:T(2,128)S(1)} %get-tuple-element.51.refs_0_), channel_id=1, source_target_pairs={{0,1},{1,0},{2,3},{3,2},{4,5},{5,4},{6,7},{7,6},{8,9},{9,8},{10,11... | collective-permute-start | bytes 3080 | tf_op jit(solution)/shard_map/ppermute | solution.py:616
  13.3 7.3 %collective-permute-start.3 = (f32[168,256]{1,0:T(8,128)S(1)}, f32[168,256]{1,0:T(8,128)S(1)}, u32[]{:S(2)}, u32[]{:S(2)}) collective-permute-start(f32[168,256]{1,0:T(8,128)S(1)} %get-tuple-element.58.send_a_ref), channel_id=1, source_target_pairs={{0,4},{4,0},{8,12},{12,8},{16,20},{20,16},{24,28},{28,24},{1,5},{5... | collective-permute-start | bytes 516104 | tf_op jit(solution)/shard_map/ppermute | solution.py:477
  15.3 8.6 %collective-permute-start.8 = (f32[168,256]{1,0:T(8,128)S(1)}, f32[168,256]{1,0:T(8,128)S(1)}, u32[]{:S(2)}, u32[]{:S(2)}) collective-permute-start(f32[168,256]{1,0:T(8,128)S(1)} %get-tuple-element.77), channel_id=1, source_target_pairs={{0,4},{4,0},{8,12},{12,8},{16,20},{20,16},{24,28},{28,24},{1,5},{5... | collective-permute-start | bytes 516104 | tf_op jit(solution)/shard_map/ppermute | solution.py:477
  20.7 7.6 %collective-permute-start.5 = (f32[168,256]{1,0:T(8,128)S(1)}, f32[168,256]{1,0:T(8,128)S(1)}, u32[]{:S(2)}, u32[]{:S(2)}) collective-permute-start(f32[168,256]{1,0:T(8,128)S(1)} %join.6.sum0), channel_id=1, source_target_pairs={{0,8},{4,12},{8,0},{12,4},{16,24},{20,28},{24,16},{28,20},{1,9},{5... | collective-permute-start | bytes 516104 | tf_op jit(solution)/shard_map/ppermute | solution.py:511
  22.3 6.0 %collective-permute-start.4 = (f32[152,256]{1,0:T(8,128)S(1)}, f32[152,256]{1,0:T(8,128)S(1)}, u32[]{:S(2)}, u32[]{:S(2)}) collective-permute-start(f32[152,256]{1,0:T(8,128)S(1)} %get-tuple-element.66), channel_id=1, source_target_pairs={{0,4},{4,0},{8,12},{12,8},{16,20},{20,16},{24,28},{28,24},{1,5},{5... | collective-permute-start | bytes 466952 | tf_op jit(solution)/shard_map/ppermute | solution.py:477
  23.9 7.5 %collective-permute-start.9 = (f32[152,256]{1,0:T(8,128)S(1)}, f32[152,256]{1,0:T(8,128)S(1)}, u32[]{:S(2)}, u32[]{:S(2)}) collective-permute-start(f32[152,256]{1,0:T(8,128)S(1)} %get-tuple-element.78), channel_id=1, source_target_pairs={{0,4},{4,0},{8,12},{12,8},{16,20},{20,16},{24,28},{28,24},{1,5},{5... | collective-permute-start | bytes 466952 | tf_op jit(solution)/shard_map/ppermute | solution.py:477
  25.5 6.6 %collective-permute-start.10 = (f32[168,256]{1,0:T(8,128)S(1)}, f32[168,256]{1,0:T(8,128)S(1)}, u32[]{:S(2)}, u32[]{:S(2)}) collective-permute-start(f32[168,256]{1,0:T(8,128)S(1)} %join.8.sum0), channel_id=1, source_target_pairs={{0,8},{4,12},{8,0},{12,4},{16,24},{20,28},{24,16},{28,20},{1,9},{5... | collective-permute-start | bytes 516104 | tf_op jit(solution)/shard_map/ppermute | solution.py:511
  28.3 6.8 %collective-permute-start.6 = (f32[152,256]{1,0:T(8,128)S(1)}, f32[152,256]{1,0:T(8,128)S(1)}, u32[]{:S(2)}, u32[]{:S(2)}) collective-permute-start(f32[152,256]{1,0:T(8,128)S(1)} %get-tuple-element.70), channel_id=1, source_target_pairs={{0,4},{4,0},{8,12},{12,8},{16,20},{20,16},{24,28},{28,24},{1,5},{5... | collective-permute-start | bytes 466952 | tf_op jit(solution)/shard_map/ppermute | solution.py:477
  29.9 5.7 %collective-permute-start.16 = (f32[152,256]{1,0:T(8,128)S(1)}, f32[152,256]{1,0:T(8,128)S(1)}, u32[]{:S(2)}, u32[]{:S(2)}) collective-permute-start(f32[152,256]{1,0:T(8,128)S(1)} %get-tuple-element.90.sum1), channel_id=1, source_target_pairs={{0,8},{4,12},{8,0},{12,4},{16,24},{20,28},{24,16},{28,20},{1,9},{5... | collective-permute-start | bytes 466952 | tf_op jit(solution)/shard_map/ppermute | solution.py:515
  31.4 5.4 %collective-permute-start.17 = (f32[168,256]{1,0:T(8,128)S(1)}, f32[168,256]{1,0:T(8,128)S(1)}, u32[]{:S(2)}, u32[]{:S(2)}) collective-permute-start(f32[168,256]{1,0:T(8,128)S(1)} %get-tuple-element.91.both0), channel_id=1, source_target_pairs={{0,1},{1,0},{2,3},{3,2},{4,5},{5,4},{6,7},{7,6},{8,16},{9,17},{10,... | collective-permute-start | bytes 516104 | tf_op jit(solution)/shard_map/ppermute | solution.py:516
  32.1 7.3 %collective-permute-start.11 = (f32[152,256]{1,0:T(8,128)S(1)}, f32[152,256]{1,0:T(8,128)S(1)}, u32[]{:S(2)}, u32[]{:S(2)}) collective-permute-start(f32[152,256]{1,0:T(8,128)S(1)} %get-tuple-element.82), channel_id=1, source_target_pairs={{0,4},{4,0},{8,12},{12,8},{16,20},{20,16},{24,28},{28,24},{1,5},{5... | collective-permute-start | bytes 466952 | tf_op jit(solution)/shard_map/ppermute | solution.py:477
  33.1 6.3 %collective-permute-start.12 = (f32[152,256]{1,0:T(8,128)S(1)}, f32[152,256]{1,0:T(8,128)S(1)}, u32[]{:S(2)}, u32[]{:S(2)}) collective-permute-start(f32[152,256]{1,0:T(8,128)S(1)} %get-tuple-element.83.sum1), channel_id=1, source_target_pairs={{0,8},{4,12},{8,0},{12,4},{16,24},{20,28},{24,16},{28,20},{1,9},{5... | collective-permute-start | bytes 466952 | tf_op jit(solution)/shard_map/ppermute | solution.py:515
  35.1 4.3 %collective-permute-start.13 = (f32[168,256]{1,0:T(8,128)S(1)}, f32[168,256]{1,0:T(8,128)S(1)}, u32[]{:S(2)}, u32[]{:S(2)}) collective-permute-start(f32[168,256]{1,0:T(8,128)S(1)} %get-tuple-element.84.both0), channel_id=1, source_target_pairs={{0,1},{1,0},{2,3},{3,2},{4,5},{5,4},{6,7},{7,6},{8,16},{9,17},{10,... | collective-permute-start | bytes 516104 | tf_op jit(solution)/shard_map/ppermute | solution.py:516
  35.6 9.3 %collective-permute-start.7 = (f32[304,256]{1,0:T(8,128)S(1)}, f32[304,256]{1,0:T(8,128)S(1)}, u32[]{:S(2)}, u32[]{:S(2)}) collective-permute-start(f32[304,256]{1,0:T(8,128)S(1)} %get-tuple-element.71), channel_id=1, source_target_pairs={{0,4},{4,0},{8,12},{12,8},{16,20},{20,16},{24,28},{28,24},{1,5},{5... | collective-permute-start | bytes 933896 | tf_op jit(solution)/shard_map/ppermute | solution.py:477
  36.8 7.9 %collective-permute-start.18 = (f32[168,256]{1,0:T(8,128)S(1)}, f32[168,256]{1,0:T(8,128)S(1)}, u32[]{:S(2)}, u32[]{:S(2)}) collective-permute-start(f32[168,256]{1,0:T(8,128)S(1)} %get-tuple-element.92.refs_2_), channel_id=1, source_target_pairs={{0,8},{4,12},{8,0},{12,4},{16,24},{20,28},{24,16},{28,20},{1,9},{5... | collective-permute-start | bytes 516104 | tf_op jit(solution)/shard_map/ppermute | solution.py:520
  39.5 7.5 %collective-permute-start.14 = (f32[168,256]{1,0:T(8,128)S(1)}, f32[168,256]{1,0:T(8,128)S(1)}, u32[]{:S(2)}, u32[]{:S(2)}) collective-permute-start(f32[168,256]{1,0:T(8,128)S(1)} %get-tuple-element.85.refs_2_), channel_id=1, source_target_pairs={{0,8},{4,12},{8,0},{12,4},{16,24},{20,28},{24,16},{28,20},{1,9},{5... | collective-permute-start | bytes 516104 | tf_op jit(solution)/shard_map/ppermute | solution.py:520
  41.7 1.4 %collective-permute-start.19 = (f32[152,256]{1,0:T(8,128)S(1)}, f32[152,256]{1,0:T(8,128)S(1)}, u32[]{:S(2)}, u32[]{:S(2)}) collective-permute-start(f32[152,256]{1,0:T(8,128)S(1)} %get-tuple-element.93), channel_id=1, source_target_pairs={{0,1},{1,0},{2,3},{3,2},{4,5},{5,4},{6,7},{7,6},{8,16},{9,17},{10,... | collective-permute-start | bytes 466952 | tf_op jit(solution)/shard_map/ppermute | solution.py:521
  41.7 3.9 %collective-permute-start.15 = (f32[152,256]{1,0:T(8,128)S(1)}, f32[152,256]{1,0:T(8,128)S(1)}, u32[]{:S(2)}, u32[]{:S(2)}) collective-permute-start(f32[152,256]{1,0:T(8,128)S(1)} %get-tuple-element.86), channel_id=1, source_target_pairs={{0,1},{1,0},{2,3},{3,2},{4,5},{5,4},{6,7},{7,6},{8,16},{9,17},{10,... | collective-permute-start | bytes 466952 | tf_op jit(solution)/shard_map/ppermute | solution.py:521
